TPU v7x, 256 devices: a whole 4x4x8 slice. The times are simulated.
256 devices in a mesh: inp: 128 (over z_lo, x, y, core), tm: 2 (over z_hi).
Axes of the slice: x: 4, y: 4, z: 8 (z_hi: 2, z_lo: 4; z = z_hi * 4 + z_lo), core: 2. Of those that a mesh axis runs over, the one named last changes fastest.
Arguments:
- samples: bfloat16 [768, 128, 3072], P('inp', 'tm'), may hold values from -6 to 6
Outputs:
- visibilities: float32 [512, 2, 768, 768], P(('inp', 'tm'))
All inputs are finite; a program needn't handle non-finite values.
Results may differ from a plain program's by a relative error of at most 0.0095.
Values may be sent and summed in bfloat16 or wider, within the bound.
A program may use at most 128 MiB of HBM per device.

v0:
```python
import jax
import jax.numpy as jnp
from jax import lax
from jax.sharding import PartitionSpec as P

FRAME = 3072
TAPS = 4
CH = 512
FIRST = 256


def from_behind(block, axis, distance):
    devices = range(lax.axis_size(axis))
    route = [(i - distance, i) for i in devices if i - distance in devices]
    return lax.ppermute(block, axis, route)


def pfb_weights():
    total = TAPS * FRAME
    place = jnp.arange(total, dtype=jnp.float32)
    centred = (place - (total - 1) / 2.0) / FRAME
    taper = 0.5 - 0.5 * jnp.cos(2.0 * jnp.pi * (place + 0.5) / total)
    shape_vals = jnp.sinc(centred) * taper
    norm_value = jnp.sqrt(jnp.sum(shape_vals * shape_vals) / FRAME)
    return (shape_vals / norm_value).reshape(TAPS, FRAME)


def dft_table():
    sample_idx = jnp.arange(FRAME, dtype=jnp.int32)
    chan_idx = FIRST + jnp.arange(CH, dtype=jnp.int32)
    phase_idx = sample_idx[:, None] * chan_idx[None, :] % FRAME
    angle = 2.0 * jnp.pi * phase_idx.astype(jnp.float32) / FRAME
    scaling = jnp.sqrt(2.0 / FRAME)
    return (jnp.concatenate([jnp.cos(angle), -jnp.sin(angle)], axis=1) * scaling).astype(
        jnp.bfloat16
    )


def correlate(block):
    products = jnp.einsum("pcis,qcjs->cpiqj", block, block, preferred_element_type=jnp.float32)
    real_part = products[:, 0, :, 0, :] + products[:, 1, :, 1, :]
    imag_part = products[:, 1, :, 0, :] - products[:, 0, :, 1, :]
    return jnp.stack([real_part, imag_part], axis=1)


def local(samples):
    inp_dev, spec_dev, frame_len = samples.shape
    tm_count = lax.axis_size("tm")
    history = from_behind(samples[:, spec_dev - (TAPS - 1) :, :], "tm", 1)
    extended = jnp.concatenate([history, samples], axis=1).astype(jnp.float32)
    weights = pfb_weights()
    filtered = weights[0] * extended[:, 0:spec_dev, :]
    for tap_index in range(1, TAPS):
        filtered = filtered + weights[tap_index] * extended[:, tap_index : tap_index + spec_dev, :]
    filtered = filtered.astype(jnp.bfloat16)
    spectra = jnp.einsum(
        "isf,fp->pis", filtered, dft_table(), preferred_element_type=jnp.float32
    ).astype(jnp.bfloat16)
    spectra = spectra.reshape(2, CH, inp_dev, spec_dev)
    block = lax.all_to_all(
        lax.all_to_all(spectra, "inp", split_axis=1, concat_axis=2, tiled=True),
        "tm",
        split_axis=1,
        concat_axis=3,
        tiled=True,
    )
    summed = correlate(block)
    return summed * (1.0 / (spec_dev * tm_count))


def solution(mesh):
    return jax.shard_map(
        local,
        mesh=mesh,
        in_specs=(P("inp", "tm", None),),
        out_specs=P(("inp", "tm"), None, None, None),
        check_vma=False,
    )
```

profile of v0, /device:TPU:32, one launch (start us, length us, event | category | flops | bytes accessed | tf_op | source)
XLA Modules:
  0.0 130.3 jit_solution(7307827522354518536)
XLA Ops:
  0.0 1.0 slice.44
  1.0 8.2 %collective-permute-start = (bf16[6,3,3072]{2,1,0:T(4,128)(2,1)S(1)}, bf16[6,3,3072]{2,1,0:T(4,128)(2,1)S(1)}, u32[]{:S(2)}, u32[]{:S(2)}) collective-permute-start(bf16[6,3,3072]{2,1,0:T(4,128)(2,1)S(1)} %slice.44), channel_id=1, source_target_pairs={{0,1},{2,3},{4,5},{6,7},{8,9},{10,11},{12,13},{14,15},{16,17},{18,... | collective-permute-start | bytes 331784 | tf_op jit(solution)/shard_map/ppermute | solution.py:15
  9.3 0.8 multiply_reduce_fusion
  10.8 0.3 broadcast_divide_fusion
  11.1 0.0 copy-start
  11.1 27.1 %fusion.8 = (f32[3072,512]{1,0:T(8,128)}, f32[3072,512]{1,0:T(8,128)}) fusion(s32[512]{0:T(512)S(1)} %iota_add_fusion.2), kind=kLoop, calls=%fused_computation.12 | loop fusion | flops 15728640 | bytes 12584960 | tf_op jit(solution)/shard_map/cos | solution.py:34
  38.2 0.0 collective-permute-done
  38.2 0.0 copy-done
  38.2 3.2 %maximum_convert_fusion = f32[6,67,3072]{2,1,0:T(8,128)} fusion(bf16[6,64,3072]{2,1,0:T(8,128)(2,1)S(1)} %copy-done, bf16[6,3,3072]{2,1,0:T(4,128)(2,1)S(1)} %collective-permute-done), kind=kLoop, calls=%fused_computation.28 | loop fusion | flops 4939776 | bytes 7409664 | tf_op jit(solution)/shard_map/convert_element_type | solution.py:50
  41.4 14.0 %fusion.22 = bf16[1024,6,64]{0,2,1:T(8,128)(2,1)S(1)} fusion(f32[6,67,3072]{2,1,0:T(8,128)} %maximum_convert_fusion, f32[3072]{0:T(1024)S(1)} %get-tuple-element.6, f32[3072]{0:T(1024)S(1)} %get-tuple-element.7, f32[3072]{0:T(1024)S(1)} %get-tuple-element.8, f32[3072]{0:T(1024)S(1)} %get-tuple-element.5, f32[3072,512]{1,0:T(8,128)} %get-tuple-element.10, ...), kind=kOutput, calls=%fused_computation.33 | convolution fusion | flops 2435186688 | bytes 32292864 | tf_op jit(solution)/shard_map/isf,fp->pis/dot_general | solution.py:56
  55.4 0.6 reshape.56
  56.0 1.8 %copy.25 = bf16[2,512,6,64]{3,0,2,1:T(2,128)(2,1)S(1)} copy(bf16[2,512,6,64]{1,0,3,2:T(2,128)(2,1)S(1)} %reshape.56) | data formatting | bytes 1572864 | tf_op jit(solution)/shard_map/reshape | solution.py:59
  57.8 1.0 reshape.60
  58.9 33.4 %all_to_all.36 = bf16[128,2,1536]{2,1,0:T(2,128)(2,1)S(1)} all-to-all(bf16[128,2,1536]{2,1,0:T(2,128)(2,1)S(1)} %reshape.60), channel_id=1, replica_groups=mesh['inp'=128,'tm'=2] {'inp'}, dimensions={0} | all-to-all | bytes 1572864 | tf_op jit(solution)/shard_map/all_to_all | solution.py:61
  92.2 1.0 reshape.61
  93.2 0.3 copy.26
  93.5 0.5 copy.27
  94.1 0.9 copy.28
  95.0 26.2 %all_to_all.37 = bf16[2,4,768,64]{2,3,0,1:T(8,128)(2,1)S(1)} all-to-all(bf16[2,4,768,64]{2,3,0,1:T(8,128)(2,1)S(1)} %copy.28), channel_id=1, replica_groups=mesh['inp'=128,'tm'=2] {'tm'}, dimensions={1} | all-to-all | bytes 1572864 | tf_op jit(solution)/shard_map/all_to_all | solution.py:60
  121.2 0.1 copy.30
  121.2 2.6 %fusion.27 = f32[2,2,768,2,768]{4,2,3,1,0:T(8,128)S(1)} fusion(bf16[2,2,768,128,1]{2,3,1,0,4:T(8,128)(2,1)S(1)} %bitcast.34), kind=kOutput, calls=%fused_computation.34 | convolution fusion | flops 1207959552 | bytes 19660800 | tf_op jit(solution)/shard_map/pcis,qcjs->cpiqj/dot_general | solution.py:40
  123.9 0.6 fusion.10
  124.5 0.6 fusion.12
  125.1 0.9 maximum_multiply_fusion.1
  126.0 4.4 %copy.35 = f32[2,2,768,768]{3,2,1,0:T(8,128)} copy(f32[2,2,768,768]{3,2,0,1:T(8,128)S(1)} %maximum_multiply_fusion.1) | data formatting | bytes 18874368 | tf_op jit(solution)/shard_map/mul | solution.py:68
  (2 shorter events, 0.0 us)
Async XLA Ops:
  1.0 37.2 %collective-permute-start = (bf16[6,3,3072]{2,1,0:T(4,128)(2,1)S(1)}, bf16[6,3,3072]{2,1,0:T(4,128)(2,1)S(1)}, u32[]{:S(2)}, u32[]{:S(2)}) collective-permute-start(bf16[6,3,3072]{2,1,0:T(4,128)(2,1)S(1)} %slice.44), channel_id=1, source_target_pairs={{0,1},{2,3},{4,5},{6,7},{8,9},{10,11},{12,13},{14,15},{16,17},{18,... | collective-permute-start | bytes 331784 | tf_op jit(solution)/shard_map/ppermute | solution.py:15
  11.1 27.2 %copy-start = (bf16[6,64,3072]{2,1,0:T(8,128)(2,1)S(1)}, bf16[6,64,3072]{2,1,0:T(8,128)(2,1)}, u32[]{:S(2)}) copy-start(bf16[6,64,3072]{2,1,0:T(8,128)(2,1)} %param.1) | copy-start | bytes 7077892
where the time goes:
time: 131 us; the launch traced here: 130 us
  blocking collectives  59.6 us (45%)
  other arithmetic  33.5 us (26%)
  matrix products  16.6 us (13%)
  local copies, waits for them, and re-layouts  11.6 us (9%)
  starting transfers between devices  8.2 us (6%)
    all_to_all x1, blocking collectives, local(): lax.all_to_all(spectra, 'inp', split_axis=1, concat_axis=2, tiled=True)  33.4 us
    cos x1, other arithmetic, dft_table(): jnp.cos(angle)  27.1 us
    all_to_all x1, blocking collectives, local(): lax.all_to_all(lax.all_to_all(spectra, 'inp', split_axis=1, concat_axis=2...  26.2 us
    dot_general x1, matrix products, local(): jnp.einsum('isf,fp->pis', filtered, dft_table(), preferred_element_type=j...  14 us
    ppermute x1, starting transfers between devices, from_behind(): return lax.ppermute(block, axis, route)  8.2 us
    mul x1, local copies, waits for them, and re-layouts, local(): return summed * (1.0 / (spec_dev * tm_count))  4.35 us
    convert_element_type x1, other arithmetic, local(): extended = jnp.concatenate([history, samples], axis=1).astype(jnp.float32)  3.21 us
    dot_general x1, matrix products, correlate(): jnp.einsum('pcis,qcjs->cpiqj', block, block, preferred_element_type=jnp.f...  2.65 us
  transfers between devices with their start and end apart: 1, of which 0 were waited for; matrix products, arithmetic and copies ran while one was open for 22% of the time, Pallas kernels for 0%

commit v1 on v0

v1 whole, which is shorter than its diff:
```python
import numpy as np
import jax
import jax.numpy as jnp
import ml_dtypes
from jax import lax
from jax.experimental import pallas as pl
from jax.experimental.pallas import tpu as pltpu
from jax.sharding import PartitionSpec as P

FRAME = 3072
TAPS = 4
CH = 512
FIRST = 256
MESH = pl.DeviceIdType.MESH
F32 = jnp.float32
BF16 = jnp.bfloat16
LANE_TILES = FRAME // 128
NT = (((1,), (1,)), ((), ()))


def pfb_weights():
    total = TAPS * FRAME
    place = np.arange(total, dtype=np.float64)
    centred = (place - (total - 1) / 2.0) / FRAME
    taper = 0.5 - 0.5 * np.cos(2.0 * np.pi * (place + 0.5) / total)
    vals = np.sinc(centred) * taper
    return (vals / np.sqrt(np.sum(vals * vals) / FRAME)).reshape(TAPS, FRAME).astype(np.float32)


def dft_rows():
    xd, zd, yd, cd, ch2 = np.meshgrid(
        np.arange(4), np.arange(8), np.arange(4), np.arange(2), np.arange(2), indexing="ij"
    )
    chan = (zd % 4) * 128 + xd * 32 + yd * 8 + cd * 4 + (zd // 4) * 2 + ch2
    chan = chan.reshape(4, 128)
    phase = ((chan[:, :, None] + FIRST) * np.arange(FRAME)[None, None, :]) % FRAME
    angle = 2.0 * np.pi * np.arange(FRAME) / FRAME
    scale = np.sqrt(2.0 / FRAME)
    cos = (np.cos(angle) * scale).astype(ml_dtypes.bfloat16)
    sin = (-np.sin(angle) * scale).astype(ml_dtypes.bfloat16)
    return np.concatenate([cos[phase], sin[phase]], axis=1)


def shuffle(source):
    n = source.size
    out = np.zeros((n, n), ml_dtypes.bfloat16)
    out[np.arange(n), source.reshape(-1)] = 1.0
    return out


def middle_shuffle():
    place = np.arange(384).reshape(4, 6, 8, 2)
    return shuffle(place.transpose(2, 3, 0, 1))


def final_shuffle():
    place = np.arange(384).reshape(8, 2, 4, 6)
    return shuffle(place.transpose(1, 2, 0, 3))


def turn_kernel(
    samples, table, window, perm, out,
    xs, tabs, stage, tail, filt, send, mid0, mid1, pack,
    x_sem, t_sem, z_send, z_recv, p_send, p_recv,
):
    inp = lax.axis_index("inp")
    t = lax.axis_index("tm")
    zl, xyc = inp // 32, inp % 32
    x, y, core = xyc // 8, (xyc // 2) % 4, xyc % 2
    z = t * 4 + zl

    def hop(q):
        return jnp.where(q == 0, 2, jnp.where(q == 1, 1, jnp.where(q == 2, 3, 0)))

    def z_device(place):
        return ((place % 4) * 32 + xyc, place // 4)

    def p_device(xd, yc):
        return (zl * 32 + xd * 8 + yc, t)

    for i in range(6):
        pltpu.make_async_copy(samples.at[i], xs.at[i], x_sem.at[i]).start()
    for q in range(4):
        xd = (x + hop(q)) % 4
        pltpu.make_async_copy(table.at[xd], tabs.at[q], t_sem.at[q]).start()

    barrier = pltpu.get_barrier_semaphore()
    for k in range(1, 8):
        pl.semaphore_signal(barrier, inc=1, device_id=z_device((z + k) % 8), device_id_type=MESH)
    def greet(k, _):
        other = (xyc + k) % 32
        pl.semaphore_signal(barrier, inc=1, device_id=(zl * 32 + other, t), device_id_type=MESH)
        return 0
    lax.fori_loop(1, 32, greet, 0)

    stage[:, 0:8, :] = jnp.zeros((LANE_TILES, 8, 128), F32)
    stage[:, 72:80, :] = jnp.zeros((LANE_TILES, 8, 128), F32)

    def filter_input(i, _):
        pltpu.make_async_copy(samples.at[i], xs.at[i], x_sem.at[i]).wait()
        for c in range(LANE_TILES):
            stage[c, 8:72, :] = xs[i, :, c * 128 : (c + 1) * 128].astype(F32)
        for c in range(LANE_TILES):
            cols = slice(c * 128, (c + 1) * 128)
            acc = window[0:1, cols] * stage[c, 5:77, :]
            for k in range(1, TAPS):
                acc = acc + window[k : k + 1, cols] * stage[c, 5 + k : 77 + k, :]
            filt[pl.ds(pl.multiple_of(i * 64, 64), 64), cols] = acc[0:64].astype(BF16)
            tail[pl.ds(pl.multiple_of(i * 8, 8), 8), cols] = acc[64:72]
        return 0

    lax.fori_loop(0, 6, filter_input, 0)
    filt[384:432, :] = tail[...].astype(BF16)
    filt[432:512, :] = jnp.zeros((80, FRAME), BF16)

    def z_copies(q, blocks, mid, sem):
        copies = []
        for k in range(1, 8):
            place = (z + k) % 8
            rows = pl.ds(pl.multiple_of(place * 16, 16), 16)
            copies.append(
                pltpu.make_async_remote_copy(
                    send.at[q, pl.ds(0, blocks), rows, :], mid.at[q, zl], z_send.at[q], sem.at[q],
                    device_id=z_device(place), device_id_type=MESH,
                )
            )
        rows = pl.ds(pl.multiple_of(z * 16, 16), 16)
        own = pltpu.make_async_copy(send.at[q, pl.ds(0, blocks), rows, :], mid.at[q, zl], sem.at[q])
        return copies, own

    low = lax.broadcasted_iota(jnp.int32, (128, 128), 1) < 64

    def spectra(q, _):
        pltpu.make_async_copy(table.at[0], tabs.at[q], t_sem.at[q]).wait()
        prod = lax.dot_general(tabs[q], filt[...], NT, preferred_element_type=F32)
        for pair in range(3):
            re = prod[0:128, pair * 128 : (pair + 1) * 128]
            im = prod[128:256, pair * 128 : (pair + 1) * 128]
            send[q, 2 * pair] = jnp.where(low, re, pltpu.roll(im, 64, 1)).astype(BF16)
            send[q, 2 * pair + 1] = jnp.where(low, pltpu.roll(re, 64, 1), im).astype(BF16)
        re, im = prod[0:128, 384:512], prod[128:256, 384:512]
        send[q, 6] = jnp.where(low, re, pltpu.roll(im, 64, 1)).astype(BF16)

        @pl.when(q == 0)
        def _():
            pl.semaphore_wait(barrier, 38)

        @pl.when(t == 0)
        def _():
            copies, own = z_copies(q, 7, mid0, z_recv.at[0])
            for copy in copies:
                copy.start()
            own.start()

        @pl.when(t == 1)
        def _():
            copies, own = z_copies(q, 6, mid1, z_recv.at[1])
            for copy in copies:
                copy.start()
            own.start()

        return 0

    lax.fori_loop(0, 4, spectra, 0)

    lane = lax.broadcasted_iota(jnp.int32, (16, 128), 1)
    first = (lane % 64) < TAPS - 1

    def turn(q, _):
        pltpu.make_async_copy(mid0.at[q], mid0.at[q], z_recv.at[0, q]).wait()
        pltpu.make_async_copy(mid1.at[q], mid1.at[q], z_recv.at[1, q]).wait()
        later = []
        for a in range(4):
            extra = mid0[q, a, 6].astype(F32)
            for i in range(6):
                moved = extra if i == 0 else pltpu.roll(extra, 128 - 8 * i, 1)
                later.append((mid1[q, a, i].astype(F32) + jnp.where(first, moved, 0.0)).astype(BF16))
        earlier = [mid0[q, a, i] for a in range(4) for i in range(6)]
        both = jnp.concatenate([jnp.concatenate(earlier, 0), jnp.concatenate(later, 0)], 1)
        turned = jnp.dot(perm[...], both, preferred_element_type=F32).astype(BF16)
        for yc in range(8):
            for half in range(2):
                pack[q, yc, half] = turned[yc * 48 : (yc + 1) * 48, half * 128 : (half + 1) * 128]
        xd = (x + hop(q)) % 4

        def pass_on(k, _):
            yc = (xyc + k) % 8
            pltpu.make_async_remote_copy(
                pack.at[q, yc], out.at[xyc], p_send, p_recv, device_id=p_device(xd, yc), device_id_type=MESH
            ).start()
            return 0

        @pl.when(q < 3)
        def _():
            pltpu.make_async_remote_copy(
                pack.at[q, xyc % 8], out.at[xyc], p_send, p_recv,
                device_id=p_device(xd, xyc % 8), device_id_type=MESH,
            ).start()

        @pl.when(q == 3)
        def _():
            pltpu.make_async_copy(pack.at[q, xyc % 8], out.at[xyc], p_recv).start()

        lax.fori_loop(1, 8, pass_on, 0)
        return 0

    lax.fori_loop(0, 4, turn, 0)

    pltpu.make_async_copy(out, out, p_recv).wait()

    def sent(k, _):
        pltpu.make_async_copy(pack.at[0, 0], pack.at[0, 0], p_send).wait()
        return 0

    lax.fori_loop(0, 31, sent, 0)

    def z_sent(q, _):
        @pl.when(t == 0)
        def _():
            for copy in z_copies(q, 7, mid0, z_recv.at[0])[0]:
                copy.wait_send()

        @pl.when(t == 1)
        def _():
            for copy in z_copies(q, 6, mid1, z_recv.at[1])[0]:
                copy.wait_send()

        return 0

    lax.fori_loop(0, 4, z_sent, 0)


def corner_turn(samples, table, window, perm):
    dma = pltpu.SemaphoreType.DMA
    anywhere = pl.BlockSpec(memory_space=pl.ANY)
    vmem = pl.BlockSpec(memory_space=pltpu.VMEM)
    return pl.pallas_call(
        turn_kernel,
        out_shape=jax.ShapeDtypeStruct((32, 2, 48, 128), BF16),
        in_specs=[anywhere, anywhere, vmem, vmem],
        out_specs=anywhere,
        scratch_shapes=[
            pltpu.VMEM((6, 64, FRAME), BF16),
            pltpu.VMEM((4, 256, FRAME), BF16),
            pltpu.VMEM((LANE_TILES, 80, 128), F32),
            pltpu.VMEM((48, FRAME), F32),
            pltpu.VMEM((512, FRAME), BF16),
            pltpu.VMEM((4, 7, 128, 128), BF16),
            pltpu.VMEM((4, 4, 7, 16, 128), BF16),
            pltpu.VMEM((4, 4, 6, 16, 128), BF16),
            pltpu.VMEM((4, 8, 2, 48, 128), BF16),
            dma((6,)), dma((4,)), dma((4,)), dma((2, 4)), dma, dma,
        ],
        compiler_params=pltpu.CompilerParams(
            collective_id=1, has_side_effects=True, vmem_limit_bytes=48 << 20
        ),
        name="corner_turn",
    )(samples, table, window, perm)


def correlate_kernel(turned, perm, out, left, swapped, vis, sem):
    for o in range(4):
        halves = [jnp.concatenate([turned[8 * o + k, h] for k in range(8)], 0) for h in range(2)]
        rows = jnp.dot(perm[...], jnp.concatenate(halves, 1), preferred_element_type=F32)
        low = (lax.broadcasted_iota(jnp.int32, rows.shape, 1) % 128) < 64
        parts = [pltpu.roll(rows[:, h * 128 : (h + 1) * 128], 64, 1) for h in range(2)]
        other = jnp.concatenate(parts, 1)
        other = jnp.where(low, other, -other)
        rows, other = rows.astype(BF16), other.astype(BF16)
        for ch in range(2):
            for a in range(4):
                src = slice((ch * 4 + a) * 48, (ch * 4 + a + 1) * 48)
                dst = slice(a * 192 + o * 48, a * 192 + (o + 1) * 48)
                left[ch, dst] = rows[src]
                swapped[ch, dst] = other[src]
    copies = []
    for ch in range(2):
        for part, mat in enumerate((left, swapped)):
            for r in range(3):
                block = slice(r * 256, (r + 1) * 256)
                vis[ch, part, block] = lax.dot_general(
                    mat[ch, block], left[ch], NT, preferred_element_type=F32
                ) * (1.0 / 128.0)
                copy = pltpu.make_async_copy(
                    vis.at[ch, part, pl.ds(r * 256, 256)],
                    out.at[ch, part, pl.ds(r * 256, 256)],
                    sem.at[ch, part, r],
                )
                copy.start()
                copies.append(copy)
    for copy in copies:
        copy.wait()


def correlate(turned, perm):
    vmem = pl.BlockSpec(memory_space=pltpu.VMEM)
    return pl.pallas_call(
        correlate_kernel,
        out_shape=jax.ShapeDtypeStruct((2, 2, 768, 768), F32),
        in_specs=[vmem, vmem],
        out_specs=pl.BlockSpec(memory_space=pl.ANY),
        scratch_shapes=[
            pltpu.VMEM((2, 768, 256), BF16),
            pltpu.VMEM((2, 768, 256), BF16),
            pltpu.VMEM((2, 2, 768, 768), F32),
            pltpu.SemaphoreType.DMA((2, 2, 3)),
        ],
        compiler_params=pltpu.CompilerParams(vmem_limit_bytes=48 << 20),
        name="correlate",
    )(turned, perm)


def local(samples):
    turned = corner_turn(
        samples, jnp.asarray(dft_rows()), jnp.asarray(pfb_weights()), jnp.asarray(middle_shuffle())
    )
    return correlate(turned, jnp.asarray(final_shuffle()))


def solution(mesh):
    return jax.shard_map(
        local,
        mesh=mesh,
        in_specs=(P("inp", "tm", None),),
        out_specs=P(("inp", "tm"), None, None, None),
        check_vma=False,
    )
```

time: 131 us -> 45.1 us (0.34)
  the two profiles are of different devices: /device:TPU:32 before, /device:TPU:1 now
where the time goes in v1:
time: 45.1 us; the launch traced here: 44.9 us
  Pallas kernels  41.5 us (92%)
  local copies, waits for them, and re-layouts  3.43 us (8%)
    pallas_call x1, Pallas kernels, corner_turn(): pl.pallas_call(turn_kernel, out_shape=jax.ShapeDtypeStruct((32, 2, 48, 12...  37 us
    pallas_call x1, Pallas kernels, correlate(): pl.pallas_call(correlate_kernel, out_shape=jax.ShapeDtypeStruct((2, 2, 76...  4.5 us
    unnamed x8, local copies, waits for them, and re-layouts  3.43 us

profile of v1, /device:TPU:1, one launch (start us, length us, event | category | flops | bytes accessed | tf_op | source)
XLA Modules:
  0.0 44.9 jit_solution(3156677170275084624)
XLA Ops:
  0.0 0.0 copy-start
  0.0 1.7 %copy-done = bf16[6,64,3072]{2,1,0:T(8,128)(2,1)S(1)} copy-done((bf16[6,64,3072]{2,1,0:T(8,128)(2,1)S(1)}, bf16[6,64,3072]{2,1,0:T(8,128)(2,1)}, u32[]{:S(2)}) %copy-start) | copy-done | bytes 2359320
  1.7 0.0 copy-start.1
  1.7 1.0 %copy-done.1 = bf16[384,384]{1,0:T(8,128)(2,1)S(1)} copy-done((bf16[384,384]{1,0:T(8,128)(2,1)S(1)}, bf16[384,384]{1,0:T(8,128)(2,1)}, u32[]{:S(2)}) %copy-start.1) | copy-done | bytes 294936
  2.6 0.0 copy-start.3
  2.6 0.8 %copy-done.3 = f32[4,3072]{1,0:T(4,128)S(1)} copy-done((f32[4,3072]{1,0:T(4,128)S(1)}, f32[4,3072]{1,0:T(4,128)}, u32[]{:S(2)}) %copy-start.3) | copy-done | bytes 49176
  3.4 0.0 copy-start.2
  3.4 37.0 %corner_turn.1.turned = bf16[32,2,48,128]{3,2,1,0:T(8,128)(2,1)S(1)} custom-call(bf16[6,64,3072]{2,1,0:T(8,128)(2,1)S(1)} %copy-done, bf16[4,256,3072]{2,1,0:T(8,128)(2,1)} %constant.8.clone.table, f32[4,3072]{1,0:T(4,128)S(1)} %copy-done.3, bf16[384,384]{1,0:T(8,128)(2,1)S(1)} %copy-done.1), custom_call_target="tpu_custom_call" | custom-call | tf_op jit(solution)/shard_map/corner_turn/pallas_call | solution.py:237
  40.4 0.0 copy-done.2
  40.4 4.5 %correlate.1 = f32[2,2,768,768]{3,2,1,0:T(8,128)} custom-call(bf16[32,2,48,128]{3,2,1,0:T(8,128)(2,1)S(1)} %corner_turn.1.turned, bf16[384,384]{1,0:T(8,128)(2,1)S(1)} %copy-done.2), custom_call_target="tpu_custom_call" | custom-call | tf_op jit(solution)/shard_map/correlate/pallas_call | solution.py:297
Async XLA Ops:
  0.0 1.7 %copy-start = (bf16[6,64,3072]{2,1,0:T(8,128)(2,1)S(1)}, bf16[6,64,3072]{2,1,0:T(8,128)(2,1)}, u32[]{:S(2)}) copy-start(bf16[6,64,3072]{2,1,0:T(8,128)(2,1)} %samples.1) | copy-start | bytes 7077892
  1.7 1.0 %copy-start.1 = (bf16[384,384]{1,0:T(8,128)(2,1)S(1)}, bf16[384,384]{1,0:T(8,128)(2,1)}, u32[]{:S(2)}) copy-start(bf16[384,384]{1,0:T(8,128)(2,1)} %constant.10.clone.perm) | copy-start | bytes 884740
  2.6 0.8 %copy-start.3 = (f32[4,3072]{1,0:T(4,128)S(1)}, f32[4,3072]{1,0:T(4,128)}, u32[]{:S(2)}) copy-start(f32[4,3072]{1,0:T(4,128)} %constant.9.clone.window) | copy-start | bytes 147460
  3.4 37.0 %copy-start.2 = (bf16[384,384]{1,0:T(8,128)(2,1)S(1)}, bf16[384,384]{1,0:T(8,128)(2,1)}, u32[]{:S(2)}) copy-start(bf16[384,384]{1,0:T(8,128)(2,1)} %constant.11.clone.perm) | copy-start | bytes 884740

commit v2 on v1

--- a/solution.py
+++ b/solution.py
@@ -15,6 +15,7 @@
 F32 = jnp.float32
 BF16 = jnp.bfloat16
 LANE_TILES = FRAME // 128
+RING = (4, 3, 5, 2, 6, 1, 7)
 NT = (((1,), (1,)), ((), ()))
 
 
@@ -59,9 +60,9 @@
 
 
 def turn_kernel(
-    samples, table, window, perm, out,
-    xs, tabs, stage, tail, filt, send, mid0, mid1, pack,
-    x_sem, t_sem, z_send, z_recv, p_send, p_recv,
+    samples, table, window_hbm, perm_hbm, out,
+    xs, tabs, window, perm, stage, tail, filt, extras, send, mid0, mid1, pack,
+    x_sem, t_sem, w_sem, z_send, z_recv, p_send, p_recv,
 ):
     inp = lax.axis_index("inp")
     t = lax.axis_index("tm")
@@ -80,12 +81,15 @@
 
     for i in range(6):
         pltpu.make_async_copy(samples.at[i], xs.at[i], x_sem.at[i]).start()
+    pltpu.make_async_copy(window_hbm, window, w_sem.at[0]).start()
     for q in range(4):
         xd = (x + hop(q)) % 4
         pltpu.make_async_copy(table.at[xd], tabs.at[q], t_sem.at[q]).start()
 
+    pltpu.make_async_copy(perm_hbm, perm, w_sem.at[1]).start()
+
     barrier = pltpu.get_barrier_semaphore()
-    for k in range(1, 8):
+    for k in RING:
         pl.semaphore_signal(barrier, inc=1, device_id=z_device((z + k) % 8), device_id_type=MESH)
     def greet(k, _):
         other = (xyc + k) % 32
@@ -95,6 +99,8 @@
 
     stage[:, 0:8, :] = jnp.zeros((LANE_TILES, 8, 128), F32)
     stage[:, 72:80, :] = jnp.zeros((LANE_TILES, 8, 128), F32)
+
+    pltpu.make_async_copy(window_hbm, window, w_sem.at[0]).wait()
 
     def filter_input(i, _):
         pltpu.make_async_copy(samples.at[i], xs.at[i], x_sem.at[i]).wait()
@@ -106,27 +112,35 @@
             for k in range(1, TAPS):
                 acc = acc + window[k : k + 1, cols] * stage[c, 5 + k : 77 + k, :]
             filt[pl.ds(pl.multiple_of(i * 64, 64), 64), cols] = acc[0:64].astype(BF16)
-            tail[pl.ds(pl.multiple_of(i * 8, 8), 8), cols] = acc[64:72]
+            tail[i, :, cols] = acc[64:72]
         return 0
 
     lax.fori_loop(0, 6, filter_input, 0)
-    filt[384:432, :] = tail[...].astype(BF16)
-    filt[432:512, :] = jnp.zeros((80, FRAME), BF16)
+    reach = [tail[i, 0 : TAPS - 1, :] for i in range(6)]
+    filt[384:416, :] = jnp.concatenate(reach + [jnp.zeros((14, FRAME), F32)], 0).astype(BF16)
+    filt[416:512, :] = jnp.zeros((96, FRAME), BF16)
+    extras[...] = jnp.zeros((128, 128), F32)
 
     def z_copies(q, blocks, mid, sem):
         copies = []
-        for k in range(1, 8):
+        for k in RING:
             place = (z + k) % 8
             rows = pl.ds(pl.multiple_of(place * 16, 16), 16)
             copies.append(
                 pltpu.make_async_remote_copy(
-                    send.at[q, pl.ds(0, blocks), rows, :], mid.at[q, zl], z_send.at[q], sem.at[q],
+                    send.at[q, pl.ds(0, blocks), rows, :], mid.at[q, zl, pl.ds(0, blocks)], z_send.at[q], sem.at[q],
                     device_id=z_device(place), device_id_type=MESH,
                 )
             )
         rows = pl.ds(pl.multiple_of(z * 16, 16), 16)
-        own = pltpu.make_async_copy(send.at[q, pl.ds(0, blocks), rows, :], mid.at[q, zl], sem.at[q])
+        own = pltpu.make_async_copy(send.at[q, pl.ds(0, blocks), rows, :], mid.at[q, zl, pl.ds(0, blocks)], sem.at[q])
         return copies, own
+
+    def send_z(q, blocks, mid, sem):
+        copies, own = z_copies(q, blocks, mid, sem)
+        for copy in copies:
+            copy.start()
+        own.start()
 
     low = lax.broadcasted_iota(jnp.int32, (128, 128), 1) < 64
 
@@ -139,42 +153,60 @@
             send[q, 2 * pair] = jnp.where(low, re, pltpu.roll(im, 64, 1)).astype(BF16)
             send[q, 2 * pair + 1] = jnp.where(low, pltpu.roll(re, 64, 1), im).astype(BF16)
         re, im = prod[0:128, 384:512], prod[128:256, 384:512]
-        send[q, 6] = jnp.where(low, re, pltpu.roll(im, 64, 1)).astype(BF16)
 
         @pl.when(q == 0)
         def _():
+            send[0, 6] = (re + pltpu.roll(im, 20, 1)).astype(BF16)
             pl.semaphore_wait(barrier, 38)
 
-        @pl.when(t == 0)
-        def _():
-            copies, own = z_copies(q, 7, mid0, z_recv.at[0])
-            for copy in copies:
-                copy.start()
-            own.start()
+        @pl.when(q > 0)
+        def _():
+            slot = (q - 1) * 40
+            extras[...] += pltpu.roll(re, slot, 1) + pltpu.roll(im, slot + 20, 1)
+
+        @pl.when((t == 0) & (q == 0))
+        def _():
+            send_z(q, 7, mid0, z_recv.at[0])
 
         @pl.when(t == 1)
         def _():
-            copies, own = z_copies(q, 6, mid1, z_recv.at[1])
-            for copy in copies:
-                copy.start()
-            own.start()
+            send_z(q, 6, mid1, z_recv.at[1])
 
         return 0
 
     lax.fori_loop(0, 4, spectra, 0)
 
+    @pl.when(t == 0)
+    def _():
+        send[1, 6] = extras[...].astype(BF16)
+        send_z(1, 7, mid0, z_recv.at[0])
+        for q in range(2, 4):
+            send_z(q, 6, mid0, z_recv.at[0])
+
     lane = lax.broadcasted_iota(jnp.int32, (16, 128), 1)
-    first = (lane % 64) < TAPS - 1
+    first = lane < TAPS - 1
+    second = (lane >= 64) & (lane < 64 + TAPS - 1)
+    pltpu.make_async_copy(perm_hbm, perm, w_sem.at[1]).wait()
 
     def turn(q, _):
-        pltpu.make_async_copy(mid0.at[q], mid0.at[q], z_recv.at[0, q]).wait()
+        @pl.when(q < 2)
+        def _():
+            pltpu.make_async_copy(mid0.at[q], mid0.at[q], z_recv.at[0, q]).wait()
+
+        @pl.when(q >= 2)
+        def _():
+            pltpu.make_async_copy(mid1.at[q], mid1.at[q], z_recv.at[0, q]).wait()
+
         pltpu.make_async_copy(mid1.at[q], mid1.at[q], z_recv.at[1, q]).wait()
         later = []
+        slot = jnp.maximum(q - 1, 0) * 40
         for a in range(4):
-            extra = mid0[q, a, 6].astype(F32)
+            extra = mid0[jnp.minimum(q, 1), a, 6].astype(F32)
             for i in range(6):
-                moved = extra if i == 0 else pltpu.roll(extra, 128 - 8 * i, 1)
-                later.append((mid1[q, a, i].astype(F32) + jnp.where(first, moved, 0.0)).astype(BF16))
+                re = pltpu.roll(extra, (128 - 3 * i - slot) % 128, 1)
+                im = pltpu.roll(extra, (172 - 3 * i - slot) % 128, 1)
+                added = jnp.where(first, re, jnp.where(second, im, 0.0))
+                later.append((mid1[q, a, i].astype(F32) + added).astype(BF16))
         earlier = [mid0[q, a, i] for a in range(4) for i in range(6)]
         both = jnp.concatenate([jnp.concatenate(earlier, 0), jnp.concatenate(later, 0)], 1)
         turned = jnp.dot(perm[...], both, preferred_element_type=F32).astype(BF16)
@@ -214,10 +246,10 @@
 
     lax.fori_loop(0, 31, sent, 0)
 
-    def z_sent(q, _):
+    for q in range(4):
         @pl.when(t == 0)
         def _():
-            for copy in z_copies(q, 7, mid0, z_recv.at[0])[0]:
+            for copy in z_copies(q, 7 if q < 2 else 6, mid0, z_recv.at[0])[0]:
                 copy.wait_send()
 
         @pl.when(t == 1)
@@ -225,56 +257,54 @@
             for copy in z_copies(q, 6, mid1, z_recv.at[1])[0]:
                 copy.wait_send()
 
-        return 0
-
-    lax.fori_loop(0, 4, z_sent, 0)
-
 
 def corner_turn(samples, table, window, perm):
     dma = pltpu.SemaphoreType.DMA
-    anywhere = pl.BlockSpec(memory_space=pl.ANY)
-    vmem = pl.BlockSpec(memory_space=pltpu.VMEM)
+    hbm = pl.BlockSpec(memory_space=pltpu.HBM)
     return pl.pallas_call(
         turn_kernel,
         out_shape=jax.ShapeDtypeStruct((32, 2, 48, 128), BF16),
-        in_specs=[anywhere, anywhere, vmem, vmem],
-        out_specs=anywhere,
+        in_specs=[hbm, hbm, hbm, hbm],
+        out_specs=pl.BlockSpec(memory_space=pl.ANY),
         scratch_shapes=[
             pltpu.VMEM((6, 64, FRAME), BF16),
             pltpu.VMEM((4, 256, FRAME), BF16),
+            pltpu.VMEM((TAPS, FRAME), F32),
+            pltpu.VMEM((384, 384), BF16),
             pltpu.VMEM((LANE_TILES, 80, 128), F32),
-            pltpu.VMEM((48, FRAME), F32),
+            pltpu.VMEM((6, 8, FRAME), F32),
             pltpu.VMEM((512, FRAME), BF16),
+            pltpu.VMEM((128, 128), F32),
             pltpu.VMEM((4, 7, 128, 128), BF16),
             pltpu.VMEM((4, 4, 7, 16, 128), BF16),
             pltpu.VMEM((4, 4, 6, 16, 128), BF16),
             pltpu.VMEM((4, 8, 2, 48, 128), BF16),
-            dma((6,)), dma((4,)), dma((4,)), dma((2, 4)), dma, dma,
+            dma((6,)), dma((4,)), dma((2,)), dma((4,)), dma((2, 4)), dma, dma,
         ],
         compiler_params=pltpu.CompilerParams(
             collective_id=1, has_side_effects=True, vmem_limit_bytes=48 << 20
         ),
         name="corner_turn",
-    )(samples, table, window, perm)
+    )(*(pltpu.with_memory_space_constraint(a, pltpu.HBM) for a in (samples, table, window, perm)))
 
 
 def correlate_kernel(turned, perm, out, left, swapped, vis, sem):
-    for o in range(4):
-        halves = [jnp.concatenate([turned[8 * o + k, h] for k in range(8)], 0) for h in range(2)]
-        rows = jnp.dot(perm[...], jnp.concatenate(halves, 1), preferred_element_type=F32)
-        low = (lax.broadcasted_iota(jnp.int32, rows.shape, 1) % 128) < 64
-        parts = [pltpu.roll(rows[:, h * 128 : (h + 1) * 128], 64, 1) for h in range(2)]
-        other = jnp.concatenate(parts, 1)
-        other = jnp.where(low, other, -other)
-        rows, other = rows.astype(BF16), other.astype(BF16)
-        for ch in range(2):
+    copies = []
+    low = (lax.broadcasted_iota(jnp.int32, (192, 256), 1) % 128) < 64
+    for ch in range(2):
+        for o in range(4):
+            halves = [jnp.concatenate([turned[8 * o + k, h] for k in range(8)], 0) for h in range(2)]
+            rows = jnp.dot(
+                perm[ch * 192 : (ch + 1) * 192], jnp.concatenate(halves, 1), preferred_element_type=F32
+            )
+            other = jnp.concatenate([pltpu.roll(rows[:, h * 128 : (h + 1) * 128], 64, 1) for h in range(2)], 1)
+            other = jnp.where(low, other, -other).astype(BF16)
+            rows = rows.astype(BF16)
             for a in range(4):
-                src = slice((ch * 4 + a) * 48, (ch * 4 + a + 1) * 48)
+                src = slice(a * 48, (a + 1) * 48)
                 dst = slice(a * 192 + o * 48, a * 192 + (o + 1) * 48)
                 left[ch, dst] = rows[src]
                 swapped[ch, dst] = other[src]
-    copies = []
-    for ch in range(2):
         for part, mat in enumerate((left, swapped)):
             for r in range(3):
                 block = slice(r * 256, (r + 1) * 256)

time: 45.1 us -> 40.6 us (0.900)
  local copies, waits for them, and re-layouts: 3.43 us -> 0.01 us
  Pallas kernels: 41.5 us -> 40.5 us
    unnamed x8 -> x2, local copies, waits for them, and re-layouts: 3.43 us -> 0.01 us
    pallas_call x1, Pallas kernels: 37 us -> 36.2 us  [corner_turn(): pl.pallas_call(turn_kernel, out_shape=jax.ShapeDtypeStruct((32, 2, 48, 12...]
where the time goes in v2:
time: 40.6 us; the launch traced here: 40.5 us
  Pallas kernels  40.5 us (100%)
    pallas_call x1, Pallas kernels, corner_turn(): pl.pallas_call(turn_kernel, out_shape=jax.ShapeDtypeStruct((32, 2, 48, 12...  36.2 us
    pallas_call x1, Pallas kernels, correlate(): pl.pallas_call(correlate_kernel, out_shape=jax.ShapeDtypeStruct((2, 2, 76...  4.35 us

profile of v2, /device:TPU:1, one launch (start us, length us, event | category | flops | bytes accessed | tf_op | source)
XLA Modules:
  0.0 40.5 jit_solution(18179174763356498620)
XLA Ops:
  0.0 0.0 copy-start
  0.0 36.2 %corner_turn.1.turned = bf16[32,2,48,128]{3,2,1,0:T(8,128)(2,1)S(1)} custom-call(bf16[6,64,3072]{2,1,0:T(8,128)(2,1)} %samples.1, bf16[4,256,3072]{2,1,0:T(8,128)(2,1)} %constant.8.clone.table, f32[4,3072]{1,0:T(4,128)} %constant.9.clone.window_hbm, bf16[384,384]{1,0:T(8,128)(2,1)} %constant.10.clone.perm_hbm), custom_call_target="tpu_custom_call" | custom-call | tf_op jit(solution)/shard_map/corner_turn/pallas_call | solution.py:264
  36.2 0.0 copy-done
  36.2 4.3 %correlate.1 = f32[2,2,768,768]{3,2,1,0:T(8,128)} custom-call(bf16[32,2,48,128]{3,2,1,0:T(8,128)(2,1)S(1)} %corner_turn.1.turned, bf16[384,384]{1,0:T(8,128)(2,1)S(1)} %copy-done), custom_call_target="tpu_custom_call" | custom-call | tf_op jit(solution)/shard_map/correlate/pallas_call | solution.py:327
Async XLA Ops:
  0.0 36.2 %copy-start = (bf16[384,384]{1,0:T(8,128)(2,1)S(1)}, bf16[384,384]{1,0:T(8,128)(2,1)}, u32[]{:S(2)}) copy-start(bf16[384,384]{1,0:T(8,128)(2,1)} %constant.11.clone.perm) | copy-start | bytes 884740

commit v3 on v2

--- a/solution.py
+++ b/solution.py
@@ -15,6 +15,7 @@
 F32 = jnp.float32
 BF16 = jnp.bfloat16
 LANE_TILES = FRAME // 128
+HOPS = (2, 1, 3, 0)
 RING = (4, 3, 5, 2, 6, 1, 7)
 NT = (((1,), (1,)), ((), ()))
 
@@ -66,36 +67,53 @@
 ):
     inp = lax.axis_index("inp")
     t = lax.axis_index("tm")
-    zl, xyc = inp // 32, inp % 32
-    x, y, core = xyc // 8, (xyc // 2) % 4, xyc % 2
+    zl = inp // 32
+    xyc = inp - zl * 32
+    x = xyc // 8
+    yc = xyc - x * 8
+    y = yc // 2
+    core = yc - y * 2
     z = t * 4 + zl
 
-    def hop(q):
-        return jnp.where(q == 0, 2, jnp.where(q == 1, 1, jnp.where(q == 2, 3, 0)))
+    def wrap(value, size):
+        return jnp.where(value >= size, value - size, value)
+
+    xs_there = [wrap(x + k, 4) for k in range(4)]
+    ycs_there = [2 * wrap(y + k, 4) + c for k in range(4) for c in (core, 1 - core)]
+
+    def chunk_x(q):
+        there = xs_there[HOPS[3]]
+        for k in range(3):
+            there = jnp.where(q == k, xs_there[HOPS[k]], there)
+        return there
 
     def z_device(place):
-        return ((place % 4) * 32 + xyc, place // 4)
-
-    def p_device(xd, yc):
-        return (zl * 32 + xd * 8 + yc, t)
-
-    for i in range(6):
+        half = jnp.where(place >= 4, 1, 0)
+        return ((place - half * 4) * 32 + xyc, half)
+
+    def p_device(xd, there):
+        return (zl * 32 + xd * 8 + there, t)
+
+    barrier = pltpu.get_barrier_semaphore()
+    for k in RING:
+        pl.semaphore_signal(barrier, inc=1, device_id=z_device(wrap(z + k, 8)), device_id_type=MESH)
+
+    def fetch_table(q):
+        pltpu.make_async_copy(table.at[chunk_x(q)], tabs.at[q], t_sem.at[q]).start()
+
+    for i in range(2):
         pltpu.make_async_copy(samples.at[i], xs.at[i], x_sem.at[i]).start()
     pltpu.make_async_copy(window_hbm, window, w_sem.at[0]).start()
-    for q in range(4):
-        xd = (x + hop(q)) % 4
-        pltpu.make_async_copy(table.at[xd], tabs.at[q], t_sem.at[q]).start()
-
-    pltpu.make_async_copy(perm_hbm, perm, w_sem.at[1]).start()
-
-    barrier = pltpu.get_barrier_semaphore()
-    for k in RING:
-        pl.semaphore_signal(barrier, inc=1, device_id=z_device((z + k) % 8), device_id_type=MESH)
-    def greet(k, _):
-        other = (xyc + k) % 32
-        pl.semaphore_signal(barrier, inc=1, device_id=(zl * 32 + other, t), device_id_type=MESH)
-        return 0
-    lax.fori_loop(1, 32, greet, 0)
+    fetch_table(0)
+    for i in range(2, 6):
+        pltpu.make_async_copy(samples.at[i], xs.at[i], x_sem.at[i]).start()
+
+    for k in HOPS:
+        for n, there in enumerate(ycs_there):
+            if k or n:
+                pl.semaphore_signal(
+                    barrier, inc=1, device_id=p_device(xs_there[k], there), device_id_type=MESH
+                )
 
     stage[:, 0:8, :] = jnp.zeros((LANE_TILES, 8, 128), F32)
     stage[:, 72:80, :] = jnp.zeros((LANE_TILES, 8, 128), F32)
@@ -115,73 +133,113 @@
             tail[i, :, cols] = acc[64:72]
         return 0
 
-    lax.fori_loop(0, 6, filter_input, 0)
-    reach = [tail[i, 0 : TAPS - 1, :] for i in range(6)]
-    filt[384:416, :] = jnp.concatenate(reach + [jnp.zeros((14, FRAME), F32)], 0).astype(BF16)
-    filt[416:512, :] = jnp.zeros((96, FRAME), BF16)
-    extras[...] = jnp.zeros((128, 128), F32)
-
-    def z_copies(q, blocks, mid, sem):
+    def z_copies(q, first, blocks, mid, sem):
         copies = []
+        span = pl.ds(first, blocks)
         for k in RING:
-            place = (z + k) % 8
+            place = wrap(z + k, 8)
             rows = pl.ds(pl.multiple_of(place * 16, 16), 16)
             copies.append(
                 pltpu.make_async_remote_copy(
-                    send.at[q, pl.ds(0, blocks), rows, :], mid.at[q, zl, pl.ds(0, blocks)], z_send.at[q], sem.at[q],
+                    send.at[q, span, rows, :], mid.at[q, zl, span], z_send.at[q], sem.at[q],
                     device_id=z_device(place), device_id_type=MESH,
                 )
             )
         rows = pl.ds(pl.multiple_of(z * 16, 16), 16)
-        own = pltpu.make_async_copy(send.at[q, pl.ds(0, blocks), rows, :], mid.at[q, zl, pl.ds(0, blocks)], sem.at[q])
+        own = pltpu.make_async_copy(send.at[q, span, rows, :], mid.at[q, zl, span], sem.at[q])
         return copies, own
 
-    def send_z(q, blocks, mid, sem):
-        copies, own = z_copies(q, blocks, mid, sem)
+    def send_z(q, first, blocks, mid, sem):
+        copies, own = z_copies(q, first, blocks, mid, sem)
         for copy in copies:
             copy.start()
         own.start()
 
     low = lax.broadcasted_iota(jnp.int32, (128, 128), 1) < 64
 
-    def spectra(q, _):
-        pltpu.make_async_copy(table.at[0], tabs.at[q], t_sem.at[q]).wait()
-        prod = lax.dot_general(tabs[q], filt[...], NT, preferred_element_type=F32)
-        for pair in range(3):
-            re = prod[0:128, pair * 128 : (pair + 1) * 128]
-            im = prod[128:256, pair * 128 : (pair + 1) * 128]
-            send[q, 2 * pair] = jnp.where(low, re, pltpu.roll(im, 64, 1)).astype(BF16)
-            send[q, 2 * pair + 1] = jnp.where(low, pltpu.roll(re, 64, 1), im).astype(BF16)
-        re, im = prod[0:128, 384:512], prod[128:256, 384:512]
-
-        @pl.when(q == 0)
-        def _():
-            send[0, 6] = (re + pltpu.roll(im, 20, 1)).astype(BF16)
-            pl.semaphore_wait(barrier, 38)
-
-        @pl.when(q > 0)
-        def _():
-            slot = (q - 1) * 40
-            extras[...] += pltpu.roll(re, slot, 1) + pltpu.roll(im, slot + 20, 1)
-
-        @pl.when((t == 0) & (q == 0))
-        def _():
-            send_z(q, 7, mid0, z_recv.at[0])
+    def spread(prod):
+        re, im = prod[0:128], prod[128:256]
+        even = jnp.where(low, re, pltpu.roll(im, 64, 1)).astype(BF16)
+        odd = jnp.where(low, pltpu.roll(re, 64, 1), im).astype(BF16)
+        return even, odd
+
+    def put_pair(q, pair, prod):
+        even, odd = spread(prod)
+        send[q, 2 * pair] = even
+        send[q, 2 * pair + 1] = odd
+
+    def begin(pair, _):
+        lax.fori_loop(2 * pair, 2 * pair + 2, filter_input, 0)
+
+        @pl.when(pair == 0)
+        def _():
+            for q in range(1, 4):
+                fetch_table(q)
+            pltpu.make_async_copy(perm_hbm, perm, w_sem.at[1]).start()
+            pltpu.make_async_copy(table.at[0], tabs.at[0], t_sem.at[0]).wait()
 
         @pl.when(t == 1)
         def _():
-            send_z(q, 6, mid1, z_recv.at[1])
+            rows = filt[pl.ds(pl.multiple_of(pair * 128, 128), 128), :]
+            put_pair(0, pair, lax.dot_general(tabs[0], rows, NT, preferred_element_type=F32))
+
+            @pl.when(pair == 0)
+            def _():
+                pl.semaphore_wait(barrier, 38)
+
+            send_z(0, 2 * pair, 2, mid1, z_recv.at[1])
 
         return 0
 
-    lax.fori_loop(0, 4, spectra, 0)
+    lax.fori_loop(0, 3, begin, 0)
+
+    @pl.when(t == 1)
+    def _():
+        def spectra(q, _):
+            pltpu.make_async_copy(table.at[0], tabs.at[q], t_sem.at[q]).wait()
+            prod = lax.dot_general(tabs[q], filt[0:384], NT, preferred_element_type=F32)
+            for pair in range(3):
+                put_pair(q, pair, prod[:, pair * 128 : (pair + 1) * 128])
+            send_z(q, 0, 6, mid1, z_recv.at[1])
+            return 0
+
+        lax.fori_loop(1, 4, spectra, 0)
 
     @pl.when(t == 0)
     def _():
+        reach = [tail[i, 0 : TAPS - 1, :] for i in range(6)]
+        filt[384:416, :] = jnp.concatenate(reach + [jnp.zeros((14, FRAME), F32)], 0).astype(BF16)
+        filt[416:512, :] = jnp.zeros((96, FRAME), BF16)
+
+        def spectra(q, _):
+            @pl.when(q > 0)
+            def _():
+                pltpu.make_async_copy(table.at[0], tabs.at[q], t_sem.at[q]).wait()
+
+            prod = lax.dot_general(tabs[q], filt[...], NT, preferred_element_type=F32)
+            for pair in range(3):
+                put_pair(q, pair, prod[:, pair * 128 : (pair + 1) * 128])
+            re, im = prod[0:128, 384:512], prod[128:256, 384:512]
+
+            @pl.when(q == 0)
+            def _():
+                send[0, 6] = (re + pltpu.roll(im, 20, 1)).astype(BF16)
+                extras[...] = jnp.zeros((128, 128), F32)
+                pl.semaphore_wait(barrier, 38)
+                send_z(0, 0, 7, mid0, z_recv.at[0])
+
+            @pl.when(q > 0)
+            def _():
+                slot = (q - 1) * 40
+                extras[...] += pltpu.roll(re, slot, 1) + pltpu.roll(im, slot + 20, 1)
+
+            return 0
+
+        lax.fori_loop(0, 4, spectra, 0)
         send[1, 6] = extras[...].astype(BF16)
-        send_z(1, 7, mid0, z_recv.at[0])
+        send_z(1, 0, 7, mid0, z_recv.at[0])
         for q in range(2, 4):
-            send_z(q, 6, mid0, z_recv.at[0])
+            send_z(q, 0, 6, mid0, z_recv.at[0])
 
     lane = lax.broadcasted_iota(jnp.int32, (16, 128), 1)
     first = lane < TAPS - 1
@@ -210,30 +268,27 @@
         earlier = [mid0[q, a, i] for a in range(4) for i in range(6)]
         both = jnp.concatenate([jnp.concatenate(earlier, 0), jnp.concatenate(later, 0)], 1)
         turned = jnp.dot(perm[...], both, preferred_element_type=F32).astype(BF16)
-        for yc in range(8):
+        for n in range(8):
             for half in range(2):
-                pack[q, yc, half] = turned[yc * 48 : (yc + 1) * 48, half * 128 : (half + 1) * 128]
-        xd = (x + hop(q)) % 4
-
-        def pass_on(k, _):
-            yc = (xyc + k) % 8
+                pack[q, n, half] = turned[n * 48 : (n + 1) * 48, half * 128 : (half + 1) * 128]
+        xd = chunk_x(q)
+
+        def pass_on(there):
             pltpu.make_async_remote_copy(
-                pack.at[q, yc], out.at[xyc], p_send, p_recv, device_id=p_device(xd, yc), device_id_type=MESH
+                pack.at[q, there], out.at[xyc], p_send, p_recv, device_id=p_device(xd, there), device_id_type=MESH
             ).start()
-            return 0
+
+        for n in (4, 5, 2, 3, 6, 7, 1):
+            pass_on(ycs_there[n])
 
         @pl.when(q < 3)
         def _():
-            pltpu.make_async_remote_copy(
-                pack.at[q, xyc % 8], out.at[xyc], p_send, p_recv,
-                device_id=p_device(xd, xyc % 8), device_id_type=MESH,
-            ).start()
+            pass_on(yc)
 
         @pl.when(q == 3)
         def _():
-            pltpu.make_async_copy(pack.at[q, xyc % 8], out.at[xyc], p_recv).start()
-
-        lax.fori_loop(1, 8, pass_on, 0)
+            pltpu.make_async_copy(pack.at[q, yc], out.at[xyc], p_recv).start()
+
         return 0
 
     lax.fori_loop(0, 4, turn, 0)
@@ -249,12 +304,12 @@
     for q in range(4):
         @pl.when(t == 0)
         def _():
-            for copy in z_copies(q, 7 if q < 2 else 6, mid0, z_recv.at[0])[0]:
+            for copy in z_copies(q, 0, 7 if q < 2 else 6, mid0, z_recv.at[0])[0]:
                 copy.wait_send()
 
         @pl.when(t == 1)
         def _():
-            for copy in z_copies(q, 6, mid1, z_recv.at[1])[0]:
+            for copy in z_copies(q, 0, 6, mid1, z_recv.at[1])[0]:
                 copy.wait_send()
 
 

time: 40.6 us -> 39.6 us (0.975)
  Pallas kernels: 40.5 us -> 39.5 us
    pallas_call x1, Pallas kernels: 36.2 us -> 35.2 us  [corner_turn(): pl.pallas_call(turn_kernel, out_shape=jax.ShapeDtypeStruct((32, 2, 48, 12...]
where the time goes in v3:
time: 39.6 us; the launch traced here: 39.5 us
  Pallas kernels  39.5 us (100%)
    pallas_call x1, Pallas kernels, corner_turn(): pl.pallas_call(turn_kernel, out_shape=jax.ShapeDtypeStruct((32, 2, 48, 12...  35.2 us
    pallas_call x1, Pallas kernels, correlate(): pl.pallas_call(correlate_kernel, out_shape=jax.ShapeDtypeStruct((2, 2, 76...  4.35 us

profile of v3, /device:TPU:1, one launch (start us, length us, event | category | flops | bytes accessed | tf_op | source)
XLA Modules:
  0.0 39.5 jit_solution(13002025865263803249)
XLA Ops:
  0.0 0.0 copy-start
  0.0 35.2 %corner_turn.1.turned = bf16[32,2,48,128]{3,2,1,0:T(8,128)(2,1)S(1)} custom-call(bf16[6,64,3072]{2,1,0:T(8,128)(2,1)} %samples.1, bf16[4,256,3072]{2,1,0:T(8,128)(2,1)} %constant.8.clone.table, f32[4,3072]{1,0:T(4,128)} %constant.9.clone.window_hbm, bf16[384,384]{1,0:T(8,128)(2,1)} %constant.10.clone.perm_hbm), custom_call_target="tpu_custom_call" | custom-call | tf_op jit(solution)/shard_map/corner_turn/pallas_call | solution.py:319
  35.2 0.0 copy-done
  35.2 4.4 %correlate.1 = f32[2,2,768,768]{3,2,1,0:T(8,128)} custom-call(bf16[32,2,48,128]{3,2,1,0:T(8,128)(2,1)S(1)} %corner_turn.1.turned, bf16[384,384]{1,0:T(8,128)(2,1)S(1)} %copy-done), custom_call_target="tpu_custom_call" | custom-call | tf_op jit(solution)/shard_map/correlate/pallas_call | solution.py:382
Async XLA Ops:
  0.0 35.2 %copy-start = (bf16[384,384]{1,0:T(8,128)(2,1)S(1)}, bf16[384,384]{1,0:T(8,128)(2,1)}, u32[]{:S(2)}) copy-start(bf16[384,384]{1,0:T(8,128)(2,1)} %constant.11.clone.perm) | copy-start | bytes 884740

commit v4 on v3

v4 whole, which is shorter than its diff:
```python
import numpy as np
import jax
import jax.numpy as jnp
import ml_dtypes
from jax import lax
from jax.experimental import pallas as pl
from jax.experimental.pallas import tpu as pltpu
from jax.sharding import PartitionSpec as P

FRAME = 3072
TAPS = 4
CH = 512
FIRST = 256
MESH = pl.DeviceIdType.MESH
F32 = jnp.float32
BF16 = jnp.bfloat16
LANE_TILES = FRAME // 128
GROUPS = (
    ((2, 2), (1, 2), (3, 2), (2, 1)),
    ((2, 3), (0, 2), (1, 1), (3, 3)),
    ((2, 0), (1, 3), (3, 1), (3, 0)),
    ((0, 1), (0, 3), (1, 0), (0, 0)),
)
RING = (4, 3, 5, 2, 6, 1, 7)
NT = (((1,), (1,)), ((), ()))


def pfb_weights():
    total = TAPS * FRAME
    place = np.arange(total, dtype=np.float64)
    centred = (place - (total - 1) / 2.0) / FRAME
    taper = 0.5 - 0.5 * np.cos(2.0 * np.pi * (place + 0.5) / total)
    vals = np.sinc(centred) * taper
    return (vals / np.sqrt(np.sum(vals * vals) / FRAME)).reshape(TAPS, FRAME).astype(np.float32)


def dft_rows():
    xd, yd, zd, cd, ch2 = np.meshgrid(
        np.arange(4), np.arange(4), np.arange(8), np.arange(2), np.arange(2), indexing="ij"
    )
    chan = (zd % 4) * 128 + xd * 32 + yd * 8 + cd * 4 + (zd // 4) * 2 + ch2
    chan = chan.reshape(16, 32)
    phase = ((chan[:, :, None] + FIRST) * np.arange(FRAME)[None, None, :]) % FRAME
    angle = 2.0 * np.pi * np.arange(FRAME) / FRAME
    scale = np.sqrt(2.0 / FRAME)
    cos = (np.cos(angle) * scale).astype(ml_dtypes.bfloat16)
    sin = (-np.sin(angle) * scale).astype(ml_dtypes.bfloat16)
    return np.concatenate([cos[phase], sin[phase]], axis=1)


def shuffle(source):
    n = source.size
    out = np.zeros((n, n), ml_dtypes.bfloat16)
    out[np.arange(n), source.reshape(-1)] = 1.0
    return out


def source_shuffle():
    place = np.arange(128).reshape(4, 8, 2, 2)
    return shuffle(place.transpose(1, 0, 2, 3))


def middle_shuffle():
    place = np.arange(384).reshape(4, 6, 8, 2)
    return shuffle(place.transpose(2, 3, 0, 1))


def final_shuffle():
    place = np.arange(384).reshape(8, 2, 4, 6)
    return shuffle(place.transpose(1, 2, 0, 3))


def turn_kernel(
    samples, table, window_hbm, perm_hbm, order_hbm, out,
    xs, tabs, window, perm, order, stage, tail, filt, extras, send, mid0, mid1, pack,
    x_sem, t_sem, w_sem, z_send, z_recv, p_send, p_recv,
):
    inp = lax.axis_index("inp")
    t = lax.axis_index("tm")
    zl = inp // 32
    xyc = inp - zl * 32
    x = xyc // 8
    yc = xyc - x * 8
    y = yc // 2
    core = yc - y * 2
    z = t * 4 + zl

    def wrap(value, size):
        return jnp.where(value >= size, value - size, value)

    xs_there = [wrap(x + k, 4) for k in range(4)]
    ys_there = [wrap(y + k, 4) for k in range(4)]

    def z_device(place):
        half = jnp.where(place >= 4, 1, 0)
        return ((place - half * 4) * 32 + xyc, half)

    def p_device(dx, dy, c):
        return (zl * 32 + xs_there[dx] * 8 + ys_there[dy] * 2 + c, t)

    barrier = pltpu.get_barrier_semaphore()
    for k in RING:
        pl.semaphore_signal(barrier, inc=1, device_id=z_device(wrap(z + k, 8)), device_id_type=MESH)

    def fetch_table(q):
        for k, (dx, dy) in enumerate(GROUPS[q]):
            chip = xs_there[dx] * 4 + ys_there[dy]
            pltpu.make_async_copy(table.at[chip], tabs.at[q, pl.ds(64 * k, 64)], t_sem.at[q]).start()

    for i in range(2):
        pltpu.make_async_copy(samples.at[i], xs.at[i], x_sem.at[i]).start()
    pltpu.make_async_copy(window_hbm, window, w_sem.at[0]).start()
    pltpu.make_async_copy(order_hbm, order, w_sem.at[2]).start()
    fetch_table(0)
    for i in range(2, 6):
        pltpu.make_async_copy(samples.at[i], xs.at[i], x_sem.at[i]).start()

    for group in GROUPS:
        for dx, dy in group:
            for c in (core, 1 - core):
                if dx or dy or c is not core:
                    pl.semaphore_signal(barrier, inc=1, device_id=p_device(dx, dy, c), device_id_type=MESH)

    stage[:, 0:8, :] = jnp.zeros((LANE_TILES, 8, 128), F32)
    stage[:, 72:80, :] = jnp.zeros((LANE_TILES, 8, 128), F32)

    pltpu.make_async_copy(window_hbm, window, w_sem.at[0]).wait()
    pltpu.make_async_copy(order_hbm, order, w_sem.at[2]).wait()

    def filter_input(i, _):
        pltpu.make_async_copy(samples.at[i], xs.at[i], x_sem.at[i]).wait()
        for c in range(LANE_TILES):
            stage[c, 8:72, :] = xs[i, :, c * 128 : (c + 1) * 128].astype(F32)
        for c in range(LANE_TILES):
            cols = slice(c * 128, (c + 1) * 128)
            acc = window[0:1, cols] * stage[c, 5:77, :]
            for k in range(1, TAPS):
                acc = acc + window[k : k + 1, cols] * stage[c, 5 + k : 77 + k, :]
            filt[pl.ds(pl.multiple_of(i * 64, 64), 64), cols] = acc[0:64].astype(BF16)
            tail[i, :, cols] = acc[64:72]
        return 0

    def z_copies(q, first, blocks, mid, sem):
        copies = []
        span = pl.ds(first, blocks)
        for k in RING:
            place = wrap(z + k, 8)
            copies.append(
                pltpu.make_async_remote_copy(
                    send.at[q, place, span], mid.at[q, zl, span], z_send.at[q], sem.at[q],
                    device_id=z_device(place), device_id_type=MESH,
                )
            )
        own = pltpu.make_async_copy(send.at[q, z, span], mid.at[q, zl, span], sem.at[q])
        return copies, own

    def send_z(q, first, blocks, mid, sem):
        copies, own = z_copies(q, first, blocks, mid, sem)
        for copy in copies:
            copy.start()
        own.start()

    low = lax.broadcasted_iota(jnp.int32, (128, 128), 1) < 64

    def parts(prod):
        re = jnp.concatenate([prod[64 * k : 64 * k + 32] for k in range(4)], 0)
        im = jnp.concatenate([prod[64 * k + 32 : 64 * k + 64] for k in range(4)], 0)
        return re, im

    def put(q, first, prod):
        blocks = []
        for n in range(prod.shape[1] // 128):
            re, im = parts(prod[:, n * 128 : (n + 1) * 128])
            blocks.append(jnp.where(low, re, pltpu.roll(im, 64, 1)).astype(BF16))
            blocks.append(jnp.where(low, pltpu.roll(re, 64, 1), im).astype(BF16))
        moved = jnp.dot(order[...], jnp.concatenate(blocks, 1), preferred_element_type=F32).astype(BF16)
        for n in range(len(blocks)):
            send[q, :, first + n] = moved[:, n * 128 : (n + 1) * 128].reshape(8, 16, 128)

    def put_extras(q, rows):
        moved = jnp.dot(order[...], rows.astype(BF16), preferred_element_type=F32).astype(BF16)
        send[q, :, 6] = moved.reshape(8, 16, 128)

    def begin(pair, _):
        lax.fori_loop(2 * pair, 2 * pair + 2, filter_input, 0)

        @pl.when(pair == 0)
        def _():
            for q in range(1, 4):
                fetch_table(q)
            pltpu.make_async_copy(perm_hbm, perm, w_sem.at[1]).start()
            pltpu.make_async_copy(tabs.at[0], tabs.at[0], t_sem.at[0]).wait()

        @pl.when(t == 1)
        def _():
            rows = filt[pl.ds(pl.multiple_of(pair * 128, 128), 128), :]
            put(0, 2 * pair, lax.dot_general(tabs[0], rows, NT, preferred_element_type=F32))

            @pl.when(pair == 0)
            def _():
                pl.semaphore_wait(barrier, 38)

            send_z(0, 2 * pair, 2, mid1, z_recv.at[1])

        return 0

    lax.fori_loop(0, 3, begin, 0)

    @pl.when(t == 1)
    def _():
        def spectra(q, _):
            pltpu.make_async_copy(tabs.at[q], tabs.at[q], t_sem.at[q]).wait()
            put(q, 0, lax.dot_general(tabs[q], filt[0:384], NT, preferred_element_type=F32))
            send_z(q, 0, 6, mid1, z_recv.at[1])
            return 0

        lax.fori_loop(1, 4, spectra, 0)

    @pl.when(t == 0)
    def _():
        reach = [tail[i, 0 : TAPS - 1, :] for i in range(6)]
        filt[384:416, :] = jnp.concatenate(reach + [jnp.zeros((14, FRAME), F32)], 0).astype(BF16)
        filt[416:512, :] = jnp.zeros((96, FRAME), BF16)

        def spectra(q, _):
            @pl.when(q > 0)
            def _():
                pltpu.make_async_copy(tabs.at[q], tabs.at[q], t_sem.at[q]).wait()

            prod = lax.dot_general(tabs[q], filt[...], NT, preferred_element_type=F32)
            put(q, 0, prod[:, 0:384])
            re, im = parts(prod[:, 384:512])

            @pl.when(q == 0)
            def _():
                put_extras(0, re + pltpu.roll(im, 20, 1))
                extras[...] = jnp.zeros((128, 128), F32)
                pl.semaphore_wait(barrier, 38)
                send_z(0, 0, 7, mid0, z_recv.at[0])

            @pl.when(q > 0)
            def _():
                slot = (q - 1) * 40
                extras[...] += pltpu.roll(re, slot, 1) + pltpu.roll(im, slot + 20, 1)

            return 0

        lax.fori_loop(0, 4, spectra, 0)
        put_extras(1, extras[...])
        send_z(1, 0, 7, mid0, z_recv.at[0])
        for q in range(2, 4):
            send_z(q, 0, 6, mid0, z_recv.at[0])

    lane = lax.broadcasted_iota(jnp.int32, (16, 128), 1)
    first = lane < TAPS - 1
    second = (lane >= 64) & (lane < 64 + TAPS - 1)
    pltpu.make_async_copy(perm_hbm, perm, w_sem.at[1]).wait()

    for q in range(4):
        arrived = mid0 if q < 2 else mid1
        pltpu.make_async_copy(arrived.at[q], arrived.at[q], z_recv.at[0, q]).wait()
        pltpu.make_async_copy(mid1.at[q], mid1.at[q], z_recv.at[1, q]).wait()
        later = []
        slot = max(q - 1, 0) * 40
        for a in range(4):
            extra = mid0[min(q, 1), a, 6].astype(F32)
            for i in range(6):
                re = pltpu.roll(extra, (128 - 3 * i - slot) % 128, 1)
                im = pltpu.roll(extra, (172 - 3 * i - slot) % 128, 1)
                added = jnp.where(first, re, jnp.where(second, im, 0.0))
                later.append((mid1[q, a, i].astype(F32) + added).astype(BF16))
        earlier = [mid0[q, a, i] for a in range(4) for i in range(6)]
        both = jnp.concatenate([jnp.concatenate(earlier, 0), jnp.concatenate(later, 0)], 1)
        turned = jnp.dot(perm[...], both, preferred_element_type=F32).astype(BF16)
        for n in range(8):
            for half in range(2):
                pack[q, n, half] = turned[n * 48 : (n + 1) * 48, half * 128 : (half + 1) * 128]
        for k, (dx, dy) in enumerate(GROUPS[q]):
            for c in (core, 1 - core):
                if dx or dy or c is not core:
                    pltpu.make_async_remote_copy(
                        pack.at[q, 2 * k + c], out.at[xyc], p_send, p_recv,
                        device_id=p_device(dx, dy, c), device_id_type=MESH,
                    ).start()
                else:
                    pltpu.make_async_copy(pack.at[q, 2 * k + c], out.at[xyc], p_recv).start()

    def z_sent(q, blocks):
        gone = send.at[q, pl.ds(0, 7), pl.ds(0, blocks)]
        pltpu.make_async_copy(gone, gone, z_send.at[q]).wait()

    @pl.when(t == 0)
    def _():
        for q in range(4):
            z_sent(q, 7 if q < 2 else 6)

    @pl.when(t == 1)
    def _():
        for q in range(4):
            z_sent(q, 6)

    gone = pack.at[pl.ds(0, 3)]
    pltpu.make_async_copy(gone, gone, p_send).wait()
    gone = pack.at[3, pl.ds(0, 7)]
    pltpu.make_async_copy(gone, gone, p_send).wait()
    pltpu.make_async_copy(out, out, p_recv).wait()


def corner_turn(samples, table, window, perm, order):
    dma = pltpu.SemaphoreType.DMA
    hbm = pl.BlockSpec(memory_space=pltpu.HBM)
    return pl.pallas_call(
        turn_kernel,
        out_shape=jax.ShapeDtypeStruct((32, 2, 48, 128), BF16),
        in_specs=[hbm] * 5,
        out_specs=pl.BlockSpec(memory_space=pl.ANY),
        scratch_shapes=[
            pltpu.VMEM((6, 64, FRAME), BF16),
            pltpu.VMEM((4, 256, FRAME), BF16),
            pltpu.VMEM((TAPS, FRAME), F32),
            pltpu.VMEM((384, 384), BF16),
            pltpu.VMEM((128, 128), BF16),
            pltpu.VMEM((LANE_TILES, 80, 128), F32),
            pltpu.VMEM((6, 8, FRAME), F32),
            pltpu.VMEM((512, FRAME), BF16),
            pltpu.VMEM((128, 128), F32),
            pltpu.VMEM((4, 8, 7, 16, 128), BF16),
            pltpu.VMEM((4, 4, 7, 16, 128), BF16),
            pltpu.VMEM((4, 4, 6, 16, 128), BF16),
            pltpu.VMEM((4, 8, 2, 48, 128), BF16),
            dma((6,)), dma((4,)), dma((3,)), dma((4,)), dma((2, 4)), dma, dma,
        ],
        compiler_params=pltpu.CompilerParams(
            collective_id=1, has_side_effects=True, vmem_limit_bytes=48 << 20
        ),
        name="corner_turn",
    )(*(pltpu.with_memory_space_constraint(a, pltpu.HBM) for a in (samples, table, window, perm, order)))


def correlate_kernel(turned, perm, out, left, swapped, vis, sem):
    copies = []
    low = (lax.broadcasted_iota(jnp.int32, (192, 256), 1) % 128) < 64
    for ch in range(2):
        sorted_rows = []
        for o in range(4):
            halves = [jnp.concatenate([turned[8 * o + k, h] for k in range(8)], 0) for h in range(2)]
            rows = jnp.dot(
                perm[ch * 192 : (ch + 1) * 192], jnp.concatenate(halves, 1), preferred_element_type=F32
            )
            sorted_rows.append(rows)
            for a in range(4):
                left[ch, a * 192 + o * 48 : a * 192 + (o + 1) * 48] = rows[a * 48 : (a + 1) * 48].astype(BF16)
        for part, mat in enumerate((left, swapped)):
            if part:
                for o, rows in enumerate(sorted_rows):
                    other = [pltpu.roll(rows[:, h * 128 : (h + 1) * 128], 64, 1) for h in range(2)]
                    other = jnp.concatenate(other, 1)
                    other = jnp.where(low, other, -other).astype(BF16)
                    for a in range(4):
                        swapped[ch, a * 192 + o * 48 : a * 192 + (o + 1) * 48] = other[a * 48 : (a + 1) * 48]
            for r in range(3):
                block = slice(r * 256, (r + 1) * 256)
                vis[ch, part, block] = lax.dot_general(
                    mat[ch, block], left[ch], NT, preferred_element_type=F32
                ) * (1.0 / 128.0)
                copy = pltpu.make_async_copy(
                    vis.at[ch, part, pl.ds(r * 256, 256)],
                    out.at[ch, part, pl.ds(r * 256, 256)],
                    sem.at[ch, part, r],
                )
                copy.start()
                copies.append(copy)
    for copy in copies:
        copy.wait()


def correlate(turned, perm):
    vmem = pl.BlockSpec(memory_space=pltpu.VMEM)
    return pl.pallas_call(
        correlate_kernel,
        out_shape=jax.ShapeDtypeStruct((2, 2, 768, 768), F32),
        in_specs=[vmem, vmem],
        out_specs=pl.BlockSpec(memory_space=pl.ANY),
        scratch_shapes=[
            pltpu.VMEM((2, 768, 256), BF16),
            pltpu.VMEM((2, 768, 256), BF16),
            pltpu.VMEM((2, 2, 768, 768), F32),
            pltpu.SemaphoreType.DMA((2, 2, 3)),
        ],
        compiler_params=pltpu.CompilerParams(vmem_limit_bytes=48 << 20),
        name="correlate",
    )(turned, perm)


def local(samples):
    turned = corner_turn(
        samples,
        jnp.asarray(dft_rows()),
        jnp.asarray(pfb_weights()),
        jnp.asarray(middle_shuffle()),
        jnp.asarray(source_shuffle()),
    )
    return correlate(turned, jnp.asarray(final_shuffle()))


def solution(mesh):
    return jax.shard_map(
        local,
        mesh=mesh,
        in_specs=(P("inp", "tm", None),),
        out_specs=P(("inp", "tm"), None, None, None),
        check_vma=False,
    )
```

time: 39.6 us -> 39.1 us (0.987)
  Pallas kernels: 39.5 us -> 39 us
    pallas_call x1, Pallas kernels: 35.2 us -> 34.6 us  [corner_turn(): pl.pallas_call(turn_kernel, out_shape=jax.ShapeDtypeStruct((32, 2, 48, 12...]
where the time goes in v4:
time: 39.1 us; the launch traced here: 39 us
  Pallas kernels  39 us (100%)
    pallas_call x1, Pallas kernels, corner_turn(): pl.pallas_call(turn_kernel, out_shape=jax.ShapeDtypeStruct((32, 2, 48, 12...  34.6 us
    pallas_call x1, Pallas kernels, correlate(): pl.pallas_call(correlate_kernel, out_shape=jax.ShapeDtypeStruct((2, 2, 76...  4.35 us

profile of v4, /device:TPU:1, one launch (start us, length us, event | category | flops | bytes accessed | tf_op | source)
XLA Modules:
  0.0 39.0 jit_solution(4974880720362714584)
XLA Ops:
  0.0 0.0 copy-start
  0.0 34.6 %corner_turn.1.turned = bf16[32,2,48,128]{3,2,1,0:T(8,128)(2,1)S(1)} custom-call(bf16[6,64,3072]{2,1,0:T(8,128)(2,1)} %samples.1, bf16[16,64,3072]{2,1,0:T(8,128)(2,1)} %constant.10.clone.table, f32[4,3072]{1,0:T(4,128)} %constant.11.clone.window_hbm, bf16[384,384]{1,0:T(8,128)(2,1)} %constant.12.clone.perm_hbm, bf16[128,128]{1,0:T(8,128)(2,1)} %constant.13.clone.order_hbm), custom_call_target="tpu_custom_call" | custom-call | tf_op jit(solution)/shard_map/corner_turn/pallas_call | solution.py:312
  34.6 0.0 copy-done
  34.7 4.3 %correlate.1 = f32[2,2,768,768]{3,2,1,0:T(8,128)} custom-call(bf16[32,2,48,128]{3,2,1,0:T(8,128)(2,1)S(1)} %corner_turn.1.turned, bf16[384,384]{1,0:T(8,128)(2,1)S(1)} %copy-done), custom_call_target="tpu_custom_call" | custom-call | tf_op jit(solution)/shard_map/correlate/pallas_call | solution.py:379
Async XLA Ops:
  0.0 34.6 %copy-start = (bf16[384,384]{1,0:T(8,128)(2,1)S(1)}, bf16[384,384]{1,0:T(8,128)(2,1)}, u32[]{:S(2)}) copy-start(bf16[384,384]{1,0:T(8,128)(2,1)} %constant.14.clone.perm) | copy-start | bytes 884740

commit v5 on v4

v5 whole, which is shorter than its diff:
```python
import numpy as np
import jax
import jax.numpy as jnp
import ml_dtypes
from jax import lax
from jax.experimental import pallas as pl
from jax.experimental.pallas import tpu as pltpu
from jax.sharding import PartitionSpec as P

FRAME = 3072
TAPS = 4
CH = 512
FIRST = 256
MESH = pl.DeviceIdType.MESH
F32 = jnp.float32
BF16 = jnp.bfloat16
LANE_TILES = FRAME // 128
GROUPS = (
    ((2, 2), (2, 1), (2, 3), (3, 2)),
    ((1, 2), (2, 0), (1, 3), (3, 1)),
    ((1, 1), (3, 3), (1, 0), (3, 0)),
    ((0, 2), (0, 1), (0, 3), (0, 0)),
)
RING = (4, 3, 5, 2, 6, 1, 7)
NT = (((1,), (1,)), ((), ()))


def pfb_weights():
    total = TAPS * FRAME
    place = np.arange(total, dtype=np.float64)
    centred = (place - (total - 1) / 2.0) / FRAME
    taper = 0.5 - 0.5 * np.cos(2.0 * np.pi * (place + 0.5) / total)
    vals = np.sinc(centred) * taper
    return (vals / np.sqrt(np.sum(vals * vals) / FRAME)).reshape(TAPS, FRAME).astype(np.float32)


def dft_rows():
    xd, yd, zd, cd, ch2 = np.meshgrid(
        np.arange(4), np.arange(4), np.arange(8), np.arange(2), np.arange(2), indexing="ij"
    )
    chan = (zd % 4) * 128 + xd * 32 + yd * 8 + cd * 4 + (zd // 4) * 2 + ch2
    chan = chan.reshape(16, 32)
    phase = ((chan[:, :, None] + FIRST) * np.arange(FRAME)[None, None, :]) % FRAME
    angle = 2.0 * np.pi * np.arange(FRAME) / FRAME
    scale = np.sqrt(2.0 / FRAME)
    cos = (np.cos(angle) * scale).astype(ml_dtypes.bfloat16)
    sin = (-np.sin(angle) * scale).astype(ml_dtypes.bfloat16)
    return np.concatenate([cos[phase], sin[phase]], axis=1)


def shuffle(source, columns=None):
    source = source.reshape(-1)
    out = np.zeros((source.size, columns or source.size), ml_dtypes.bfloat16)
    out[np.arange(source.size), source] = 1.0
    return out


def final_shuffle():
    return shuffle(np.arange(384).reshape(8, 2, 4, 6).transpose(1, 2, 0, 3))


def small_matrices():
    out = np.zeros((192, 640), ml_dtypes.bfloat16)
    out[:, 0:192] = shuffle(np.arange(192).reshape(6, 8, 2, 2).transpose(2, 1, 3, 0))
    out[:128, 256:384] = shuffle(np.arange(128).reshape(4, 8, 2, 2).transpose(1, 0, 2, 3))
    for i in range(6):
        for j in range(TAPS - 1):
            out[80 + 3 * i + j, 384 + j] = 1.0
            out[100 + 3 * i + j, 384 + 64 + j] = 1.0
    for n in range(8):
        for a in range(4):
            for ch in range(2):
                out[n * 16 + a * 2 + ch, 512 + a * 16 + n * 2 + ch] = 1.0
    return out


def large_matrices():
    out = np.zeros((384, 1024), ml_dtypes.bfloat16)
    out[:, 0:384] = shuffle(np.arange(384).reshape(4, 6, 8, 2).transpose(2, 3, 0, 1))
    out[:, 384:768] = shuffle(np.arange(384).reshape(8, 4, 2, 6).transpose(1, 2, 0, 3))
    zl, ch, yc, i = np.meshgrid(np.arange(4), np.arange(2), np.arange(8), np.arange(6), indexing="ij")
    out[:, 768:896] = shuffle(yc * 16 + zl * 2 + ch, 128)
    lane = np.arange(128)[None, :]
    start = 80 + 3 * i.reshape(-1, 1)
    own = (lane >= start) & (lane < start + TAPS - 1)
    own |= (lane >= start + 20) & (lane < start + 20 + TAPS - 1)
    out[:, 896:1024] = own
    return out


def turn_kernel(
    samples, table, window_hbm, large_hbm, small_hbm, out, last, added_out,
    xs, tabs, window, large, small, stage, tail, filt, extras, send, mid0, mid1, pack,
    send3, mid3, pack3, pack_e, mid_e, expanded,
    x_sem, t_sem, w_sem, z_send, z_recv, p_send, p_recv, s_sem, r_sem,
):
    inp = lax.axis_index("inp")
    t = lax.axis_index("tm")
    zl = inp // 32
    xyc = inp - zl * 32
    x = xyc // 8
    yc = xyc - x * 8
    y = yc // 2
    core = yc - y * 2
    z = t * 4 + zl

    def wrap(value, size):
        return jnp.where(value >= size, value - size, value)

    xs_there = [wrap(x + k, 4) for k in range(4)]
    ys_there = [wrap(y + k, 4) for k in range(4)]

    def z_device(place):
        half = jnp.where(place >= 4, 1, 0)
        return ((place - half * 4) * 32 + xyc, half)

    def p_device(dx, dy, c):
        return (zl * 32 + xs_there[dx] * 8 + ys_there[dy] * 2 + c, t)

    z_others = [(1 - t) * 4 + wrap(zl + k, 4) for k in range(4)]
    z_others += [t * 4 + wrap(zl + k, 4) for k in (2, 1, 3)]

    barrier = pltpu.get_barrier_semaphore()
    for k in RING:
        pl.semaphore_signal(barrier, inc=1, device_id=z_device(wrap(z + k, 8)), device_id_type=MESH)

    def fetch_table(q):
        for k, (dx, dy) in enumerate(GROUPS[q]):
            chip = xs_there[dx] * 4 + ys_there[dy]
            pltpu.make_async_copy(table.at[chip], tabs.at[q, pl.ds(64 * k, 64)], t_sem.at[q]).start()

    for i in range(2):
        pltpu.make_async_copy(samples.at[i], xs.at[i], x_sem.at[i]).start()
    pltpu.make_async_copy(window_hbm, window, w_sem.at[0]).start()
    pltpu.make_async_copy(small_hbm, small, w_sem.at[2]).start()
    fetch_table(0)
    for i in range(2, 6):
        pltpu.make_async_copy(samples.at[i], xs.at[i], x_sem.at[i]).start()

    for group in GROUPS:
        for dx, dy in group:
            for c in (core, 1 - core):
                if dx or dy or c is not core:
                    pl.semaphore_signal(barrier, inc=1, device_id=p_device(dx, dy, c), device_id_type=MESH)

    stage[:, 0:8, :] = jnp.zeros((LANE_TILES, 8, 128), F32)
    stage[:, 72:80, :] = jnp.zeros((LANE_TILES, 8, 128), F32)

    pltpu.make_async_copy(window_hbm, window, w_sem.at[0]).wait()
    pltpu.make_async_copy(small_hbm, small, w_sem.at[2]).wait()

    def filter_input(i, _):
        pltpu.make_async_copy(samples.at[i], xs.at[i], x_sem.at[i]).wait()
        for c in range(LANE_TILES):
            stage[c, 8:72, :] = xs[i, :, c * 128 : (c + 1) * 128].astype(F32)
        for c in range(LANE_TILES):
            cols = slice(c * 128, (c + 1) * 128)
            acc = window[0:1, cols] * stage[c, 5:77, :]
            for k in range(1, TAPS):
                acc = acc + window[k : k + 1, cols] * stage[c, 5 + k : 77 + k, :]
            filt[pl.ds(pl.multiple_of(i * 64, 64), 64), cols] = acc[0:64].astype(BF16)
            tail[i, :, cols] = acc[64:72]
        return 0

    def z_copies(q, first, blocks, mid, sem):
        copies = []
        span = pl.ds(first, blocks)
        for place in z_others:
            copies.append(
                pltpu.make_async_remote_copy(
                    send.at[q, place, span], mid.at[q, zl, span], z_send.at[q], sem.at[q],
                    device_id=z_device(place), device_id_type=MESH,
                )
            )
        own = pltpu.make_async_copy(send.at[q, z, span], mid.at[q, zl, span], sem.at[q])
        return copies, own

    def send_z(q, first, blocks, mid, sem):
        copies, own = z_copies(q, first, blocks, mid, sem)
        for copy in copies:
            copy.start()
        own.start()

    low = lax.broadcasted_iota(jnp.int32, (128, 128), 1) < 64

    def parts(prod):
        re = jnp.concatenate([prod[64 * k : 64 * k + 32] for k in range(4)], 0)
        im = jnp.concatenate([prod[64 * k + 32 : 64 * k + 64] for k in range(4)], 0)
        return re, im

    def blocks_of(prod):
        blocks = []
        for n in range(prod.shape[1] // 128):
            re, im = parts(prod[:, n * 128 : (n + 1) * 128])
            blocks.append(jnp.where(low, re, pltpu.roll(im, 64, 1)).astype(BF16))
            blocks.append(jnp.where(low, pltpu.roll(re, 64, 1), im).astype(BF16))
        return blocks

    def put(q, first, prod):
        blocks = blocks_of(prod)
        moved = jnp.dot(small[0:128, 256:384], jnp.concatenate(blocks, 1), preferred_element_type=F32).astype(BF16)
        for n in range(len(blocks)):
            send[q, :, first + n] = moved[:, n * 128 : (n + 1) * 128].reshape(8, 16, 128)

    def to_chips(source, dest, k):
        for n, (dx, dy) in enumerate(GROUPS[3]):
            for c in (core, 1 - core):
                if dy or c is not core:
                    pltpu.make_async_remote_copy(
                        source.at[2 * n + c], dest.at[yc], s_sem.at[k], r_sem.at[k],
                        device_id=p_device(dx, dy, c), device_id_type=MESH,
                    ).start()
                else:
                    pltpu.make_async_copy(source.at[2 * n + c], dest.at[yc], r_sem.at[k]).start()

    def put_last(prod):
        blocks = blocks_of(prod)
        by_chip = [jnp.concatenate([b[32 * k : 32 * k + 32] for b in blocks], 0) for k in range(4)]
        moved = jnp.dot(small[:, 0:192], jnp.concatenate(by_chip, 1), preferred_element_type=F32).astype(BF16)
        for k in range(4):
            for c in range(2):
                send3[2 * k + c] = moved[c * 96 : (c + 1) * 96, k * 128 : (k + 1) * 128]
        to_chips(send3, mid3, 0)

    def put_extras(q, rows):
        moved = jnp.dot(small[0:128, 256:384], rows.astype(BF16), preferred_element_type=F32).astype(BF16)
        send[q, :, 6] = moved.reshape(8, 16, 128)

    def begin(pair, _):
        lax.fori_loop(2 * pair, 2 * pair + 2, filter_input, 0)

        @pl.when(pair == 0)
        def _():
            for q in (3, 1, 2):
                fetch_table(q)
            pltpu.make_async_copy(large_hbm, large, w_sem.at[1]).start()
            pltpu.make_async_copy(tabs.at[0], tabs.at[0], t_sem.at[0]).wait()

        @pl.when(t == 1)
        def _():
            rows = filt[pl.ds(pl.multiple_of(pair * 128, 128), 128), :]
            put(0, 2 * pair, lax.dot_general(tabs[0], rows, NT, preferred_element_type=F32))

            @pl.when(pair == 0)
            def _():
                pl.semaphore_wait(barrier, 38)

            send_z(0, 2 * pair, 2, mid1, z_recv.at[1])

        return 0

    lax.fori_loop(0, 3, begin, 0)

    @pl.when(t == 1)
    def _():
        def product(q):
            pltpu.make_async_copy(tabs.at[q], tabs.at[q], t_sem.at[q]).wait()
            return lax.dot_general(tabs[q], filt[0:384], NT, preferred_element_type=F32)

        put_last(product(3))
        for q in (1, 2):
            put(q, 0, product(q))
            send_z(q, 0, 6, mid1, z_recv.at[1])

    @pl.when(t == 0)
    def _():
        reach = [tail[i, 0 : TAPS - 1, :] for i in range(6)]
        filt[384:416, :] = jnp.concatenate(reach + [jnp.zeros((14, FRAME), F32)], 0).astype(BF16)
        filt[416:512, :] = jnp.zeros((96, FRAME), BF16)

        def product(q):
            if q:
                pltpu.make_async_copy(tabs.at[q], tabs.at[q], t_sem.at[q]).wait()
            return lax.dot_general(tabs[q], filt[...], NT, preferred_element_type=F32)

        prod = product(0)
        put(0, 0, prod[:, 0:384])
        re, im = parts(prod[:, 384:512])
        put_extras(0, re + pltpu.roll(im, 20, 1))
        pl.semaphore_wait(barrier, 38)
        send_z(0, 0, 7, mid0, z_recv.at[0])
        extras[...] = jnp.zeros((128, 128), F32)
        for q in (3, 1, 2):
            prod = product(q)
            if q == 3:
                put_last(prod[:, 0:384])
            else:
                put(q, 0, prod[:, 0:384])
            re, im = parts(prod[:, 384:512])
            slot = (q - 1) * 40
            extras[...] += pltpu.roll(re, slot, 1) + pltpu.roll(im, slot + 20, 1)
        put_extras(1, extras[...])
        send_z(1, 0, 7, mid0, z_recv.at[0])
        send_z(2, 0, 6, mid0, z_recv.at[0])

    lane = lax.broadcasted_iota(jnp.int32, (16, 128), 1)
    first = lane < TAPS - 1
    second = (lane >= 64) & (lane < 64 + TAPS - 1)
    pltpu.make_async_copy(large_hbm, large, w_sem.at[1]).wait()

    for q in range(3):
        def regroup(half, blocks):
            turned = jnp.dot(large[:, 0:384], jnp.concatenate(blocks, 0), preferred_element_type=F32).astype(BF16)
            for n in range(8):
                pack[q, n, half] = turned[n * 48 : (n + 1) * 48]

        arrived = mid0 if q < 2 else mid1
        pltpu.make_async_copy(arrived.at[q], arrived.at[q], z_recv.at[0, q]).wait()
        regroup(0, [mid0[q, a, i] for a in range(4) for i in range(6)])
        slot = max(q - 1, 0) * 40
        added = []
        for a in range(4):
            extra = mid0[min(q, 1), a, 6].astype(F32)
            for i in range(6):
                re = pltpu.roll(extra, (128 - 3 * i - slot) % 128, 1)
                im = pltpu.roll(extra, (172 - 3 * i - slot) % 128, 1)
                added.append(jnp.where(first, re, jnp.where(second, im, 0.0)))
        pltpu.make_async_copy(mid1.at[q], mid1.at[q], z_recv.at[1, q]).wait()
        later = [(mid1[q, n // 6, n % 6].astype(F32) + added[n]).astype(BF16) for n in range(24)]
        regroup(1, later)
        for k, (dx, dy) in enumerate(GROUPS[q]):
            for c in (core, 1 - core):
                pltpu.make_async_remote_copy(
                    pack.at[q, 2 * k + c], out.at[xyc], p_send, p_recv,
                    device_id=p_device(dx, dy, c), device_id_type=MESH,
                ).start()

        if q == 0:
            pltpu.make_async_copy(mid3, mid3, r_sem.at[0]).wait()
            quads = [
                jnp.concatenate([mid3[n, h * 48 : (h + 1) * 48] for n in range(8)], 0) for h in range(2)
            ]
            turned = jnp.dot(large[:, 384:768], jnp.concatenate(quads, 1), preferred_element_type=F32).astype(BF16)
            for h in range(2):
                for a in range(4):
                    pack3[h * 4 + a] = turned[a * 96 : (a + 1) * 96, h * 128 : (h + 1) * 128]
            for place in z_others:
                pltpu.make_async_remote_copy(
                    pack3.at[place], last.at[z], s_sem.at[1], r_sem.at[1],
                    device_id=z_device(place), device_id_type=MESH,
                ).start()
            pltpu.make_async_copy(pack3.at[z], last.at[z], r_sem.at[1]).start()
        if q == 1:
            rows = jnp.concatenate([mid0[1, a, 6] for a in range(4)], 0)
            rows = jnp.dot(small[0:128, 512:576], rows, preferred_element_type=F32).astype(BF16)
            for n in range(8):
                pack_e[n] = rows[n * 16 : (n + 1) * 16]
            to_chips(pack_e, mid_e, 2)

    pltpu.make_async_copy(mid_e, mid_e, r_sem.at[2]).wait()
    rows = jnp.concatenate([mid_e[n] for n in range(8)], 0)
    rows = jnp.dot(large[:, 768:896], rows, preferred_element_type=F32)
    rows = jnp.where(large[:, 896:1024].astype(F32) > 0.5, rows, 0.0).astype(BF16)
    expanded[...] = jnp.dot(rows, small[0:128, 384:512], preferred_element_type=F32).astype(BF16)
    pltpu.make_async_copy(expanded, added_out, w_sem.at[3]).start()

    def all_gone(buffer, sem):
        pltpu.make_async_copy(buffer, buffer, sem).wait()

    @pl.when(t == 0)
    def _():
        for q in range(3):
            all_gone(send.at[q, pl.ds(0, 7), pl.ds(0, 7 if q < 2 else 6)], z_send.at[q])

    @pl.when(t == 1)
    def _():
        for q in range(3):
            all_gone(send.at[q, pl.ds(0, 7), pl.ds(0, 6)], z_send.at[q])

    all_gone(send3.at[pl.ds(0, 7)], s_sem.at[0])
    all_gone(pack_e.at[pl.ds(0, 7)], s_sem.at[2])
    all_gone(pack.at[pl.ds(0, 3)], p_send)
    all_gone(expanded, w_sem.at[3])
    all_gone(out.at[pl.ds(0, 24)], p_recv)
    all_gone(pack3.at[pl.ds(0, 7)], s_sem.at[1])
    all_gone(last, r_sem.at[1])


def corner_turn(samples, table, window, large, small):
    dma = pltpu.SemaphoreType.DMA
    hbm = pl.BlockSpec(memory_space=pltpu.HBM)
    anywhere = pl.BlockSpec(memory_space=pl.ANY)
    operands = (samples, table, window, large, small)
    return pl.pallas_call(
        turn_kernel,
        out_shape=(
            jax.ShapeDtypeStruct((32, 2, 48, 128), BF16),
            jax.ShapeDtypeStruct((8, 96, 128), BF16),
            jax.ShapeDtypeStruct((384, 128), BF16),
        ),
        in_specs=[hbm] * 5,
        out_specs=(anywhere, anywhere, anywhere),
        scratch_shapes=[
            pltpu.VMEM((6, 64, FRAME), BF16),
            pltpu.VMEM((4, 256, FRAME), BF16),
            pltpu.VMEM((TAPS, FRAME), F32),
            pltpu.VMEM((384, 1024), BF16),
            pltpu.VMEM((192, 640), BF16),
            pltpu.VMEM((LANE_TILES, 80, 128), F32),
            pltpu.VMEM((6, 8, FRAME), F32),
            pltpu.VMEM((512, FRAME), BF16),
            pltpu.VMEM((128, 128), F32),
            pltpu.VMEM((3, 8, 7, 16, 128), BF16),
            pltpu.VMEM((3, 4, 7, 16, 128), BF16),
            pltpu.VMEM((3, 4, 6, 16, 128), BF16),
            pltpu.VMEM((3, 8, 2, 48, 128), BF16),
            pltpu.VMEM((8, 96, 128), BF16),
            pltpu.VMEM((8, 96, 128), BF16),
            pltpu.VMEM((8, 96, 128), BF16),
            pltpu.VMEM((8, 16, 128), BF16),
            pltpu.VMEM((8, 16, 128), BF16),
            pltpu.VMEM((384, 128), BF16),
            dma((6,)), dma((4,)), dma((4,)), dma((3,)), dma((2, 3)), dma, dma, dma((3,)), dma((3,)),
        ],
        compiler_params=pltpu.CompilerParams(
            collective_id=1, has_side_effects=True, vmem_limit_bytes=48 << 20
        ),
        name="corner_turn",
    )(*(pltpu.with_memory_space_constraint(a, pltpu.HBM) for a in operands))


def correlate_kernel(turned, last, added, perm, out, left, swapped, vis, sem):
    x = (lax.axis_index("inp") // 8) % 4
    copies = []
    low = (lax.broadcasted_iota(jnp.int32, (768, 128), 1)) < 64
    for ch in range(2):
        for o in range(4):
            halves = [jnp.concatenate([turned[8 * o + k, h] for k in range(8)], 0) for h in range(2)]
            rows = jnp.dot(
                perm[ch * 192 : (ch + 1) * 192], jnp.concatenate(halves, 1), preferred_element_type=F32
            ).astype(BF16)
            for a in range(4):
                left[ch, a * 192 + o * 48 : a * 192 + (o + 1) * 48] = rows[a * 48 : (a + 1) * 48]

        for a in range(4):
            dst = pl.ds(pl.multiple_of(a * 192 + x * 48, 16), 48)
            src = slice(ch * 48, (ch + 1) * 48)
            more = added[(a * 2 + ch) * 48 : (a * 2 + ch + 1) * 48].astype(F32)
            left[ch, dst, 0:128] = last[a, src]
            left[ch, dst, 128:256] = (last[4 + a, src].astype(F32) + more).astype(BF16)
        for part, mat in enumerate((left, swapped)):
            if part:
                for h in range(2):
                    lanes = slice(h * 128, (h + 1) * 128)
                    other = pltpu.roll(left[ch, :, lanes].astype(F32), 64, 1)
                    swapped[ch, :, lanes] = jnp.where(low, other, -other).astype(BF16)
            for r in range(3):
                block = slice(r * 256, (r + 1) * 256)
                vis[ch, part, block] = lax.dot_general(
                    mat[ch, block], left[ch], NT, preferred_element_type=F32
                ) * (1.0 / 128.0)
                copy = pltpu.make_async_copy(
                    vis.at[ch, part, pl.ds(r * 256, 256)],
                    out.at[ch, part, pl.ds(r * 256, 256)],
                    sem.at[ch, part, r],
                )
                copy.start()
                copies.append(copy)
    for copy in copies:
        copy.wait()


def correlate(turned, last, added, perm):
    vmem = pl.BlockSpec(memory_space=pltpu.VMEM)
    return pl.pallas_call(
        correlate_kernel,
        out_shape=jax.ShapeDtypeStruct((2, 2, 768, 768), F32),
        in_specs=[vmem] * 4,
        out_specs=pl.BlockSpec(memory_space=pl.ANY),
        scratch_shapes=[
            pltpu.VMEM((2, 768, 256), BF16),
            pltpu.VMEM((2, 768, 256), BF16),
            pltpu.VMEM((2, 2, 768, 768), F32),
            pltpu.SemaphoreType.DMA((2, 2, 3)),
        ],
        compiler_params=pltpu.CompilerParams(vmem_limit_bytes=48 << 20),
        name="correlate",
    )(turned, last, added, perm)


def local(samples):
    turned, last, added = corner_turn(
        samples,
        jnp.asarray(dft_rows()),
        jnp.asarray(pfb_weights()),
        jnp.asarray(large_matrices()),
        jnp.asarray(small_matrices()),
    )
    return correlate(turned, last, added, jnp.asarray(final_shuffle()))


def solution(mesh):
    return jax.shard_map(
        local,
        mesh=mesh,
        in_specs=(P("inp", "tm", None),),
        out_specs=P(("inp", "tm"), None, None, None),
        check_vma=False,
    )
```

time: 39.1 us -> 37.4 us (0.957)
  Pallas kernels: 39 us -> 37.3 us
    pallas_call x1, Pallas kernels: 34.6 us -> 32.8 us  [corner_turn(): pl.pallas_call(turn_kernel, out_shape=(jax.ShapeDtypeStruct((32, 2, 48, 1...]
where the time goes in v5:
time: 37.4 us; the launch traced here: 37.3 us
  Pallas kernels  37.3 us (100%)
    pallas_call x1, Pallas kernels, corner_turn(): pl.pallas_call(turn_kernel, out_shape=(jax.ShapeDtypeStruct((32, 2, 48, 1...  32.8 us
    pallas_call x1, Pallas kernels, correlate(): pl.pallas_call(correlate_kernel, out_shape=jax.ShapeDtypeStruct((2, 2, 76...  4.45 us

profile of v5, /device:TPU:1, one launch (start us, length us, event | category | flops | bytes accessed | tf_op | source)
XLA Modules:
  0.0 37.3 jit_solution(7400733221099233946)
XLA Ops:
  0.0 0.0 copy-start
  0.0 32.8 %corner_turn.1 = (bf16[32,2,48,128]{3,2,1,0:T(8,128)(2,1)S(1)}, bf16[8,96,128]{2,1,0:T(8,128)(2,1)S(1)}, bf16[384,128]{1,0:T(8,128)(2,1)S(1)}) custom-call(bf16[6,64,3072]{2,1,0:T(8,128)(2,1)} %samples.1, bf16[16,64,3072]{2,1,0:T(8,128)(2,1)} %constant.10.clone.table, f32[4,3072]{1,0:T(4,128)} %constant.11.clone.window_hbm, ...), custom_call_target="tpu_custom_call" | custom-call | tf_op jit(solution)/shard_map/corner_turn/pallas_call | solution.py:384
  32.8 0.0 copy-done
  32.8 4.5 %correlate.1 = f32[2,2,768,768]{3,2,1,0:T(8,128)} custom-call(bf16[32,2,48,128]{3,2,1,0:T(8,128)(2,1)S(1)} %get-tuple-element.8.turned, bf16[8,96,128]{2,1,0:T(8,128)(2,1)S(1)} %get-tuple-element.9.last, bf16[384,128]{1,0:T(8,128)(2,1)S(1)} %get-tuple-element.10.added, bf16[384,384]{1,0:T(8,128)(2,1)S(1)} %copy-done), custom_call_target="tpu_custom_call" | custom-call | tf_op jit(solution)/shard_map/correlate/pallas_call | solution.py:465
Async XLA Ops:
  0.0 32.8 %copy-start = (bf16[384,384]{1,0:T(8,128)(2,1)S(1)}, bf16[384,384]{1,0:T(8,128)(2,1)}, u32[]{:S(2)}) copy-start(bf16[384,384]{1,0:T(8,128)(2,1)} %constant.14.clone.perm) | copy-start | bytes 884740

commit v6 on v5

--- a/solution.py
+++ b/solution.py
@@ -118,7 +118,11 @@
         return (zl * 32 + xs_there[dx] * 8 + ys_there[dy] * 2 + c, t)
 
     z_others = [(1 - t) * 4 + wrap(zl + k, 4) for k in range(4)]
-    z_others += [t * 4 + wrap(zl + k, 4) for k in (2, 1, 3)]
+    for spots in zip((3, 2, 1), (3, 0, 2), (0, 3, 1), (0, 1, 2)):
+        spot = spots[3]
+        for k in range(3):
+            spot = jnp.where(zl == k, spots[k], spot)
+        z_others.append(t * 4 + spot)
 
     barrier = pltpu.get_barrier_semaphore()
     for k in RING:

time: 37.4 us -> 37.8 us (1.011)
  Pallas kernels: 37.3 us -> 37.7 us
    pallas_call x1, Pallas kernels: 32.8 us -> 33.3 us  [corner_turn(): pl.pallas_call(turn_kernel, out_shape=(jax.ShapeDtypeStruct((32, 2, 48, 1...]
where the time goes in v6:
time: 37.8 us
  Pallas kernels  37.7 us (100%)
    pallas_call x1, Pallas kernels, corner_turn(): pl.pallas_call(turn_kernel, out_shape=(jax.ShapeDtypeStruct((32, 2, 48, 1...  33.3 us
    pallas_call x1, Pallas kernels, correlate(): pl.pallas_call(correlate_kernel, out_shape=jax.ShapeDtypeStruct((2, 2, 76...  4.46 us

profile of v6, /device:TPU:1, one launch (start us, length us, event | category | flops | bytes accessed | tf_op | source)
XLA Modules:
  0.0 37.8 jit_solution(10632427933973079870)
XLA Ops:
  0.0 0.0 copy-start
  0.0 33.3 %corner_turn.1 = (bf16[32,2,48,128]{3,2,1,0:T(8,128)(2,1)S(1)}, bf16[8,96,128]{2,1,0:T(8,128)(2,1)S(1)}, bf16[384,128]{1,0:T(8,128)(2,1)S(1)}) custom-call(bf16[6,64,3072]{2,1,0:T(8,128)(2,1)} %samples.1, bf16[16,64,3072]{2,1,0:T(8,128)(2,1)} %constant.10.clone.table, f32[4,3072]{1,0:T(4,128)} %constant.11.clone.window_hbm, ...), custom_call_target="tpu_custom_call" | custom-call | tf_op jit(solution)/shard_map/corner_turn/pallas_call | solution.py:388
  33.3 0.0 copy-done
  33.3 4.5 %correlate.1 = f32[2,2,768,768]{3,2,1,0:T(8,128)} custom-call(bf16[32,2,48,128]{3,2,1,0:T(8,128)(2,1)S(1)} %get-tuple-element.8.turned, bf16[8,96,128]{2,1,0:T(8,128)(2,1)S(1)} %get-tuple-element.9.last, bf16[384,128]{1,0:T(8,128)(2,1)S(1)} %get-tuple-element.10.added, bf16[384,384]{1,0:T(8,128)(2,1)S(1)} %copy-done), custom_call_target="tpu_custom_call" | custom-call | tf_op jit(solution)/shard_map/correlate/pallas_call | solution.py:469
Async XLA Ops:
  0.0 33.3 %copy-start = (bf16[384,384]{1,0:T(8,128)(2,1)S(1)}, bf16[384,384]{1,0:T(8,128)(2,1)}, u32[]{:S(2)}) copy-start(bf16[384,384]{1,0:T(8,128)(2,1)} %constant.14.clone.perm) | copy-start | bytes 884740
